TPU v7x, 256 devices: a whole 4x4x8 slice. The times are simulated.
256 devices in a mesh: ha: 16 (over y_lo, x, core), wa: 16 (over y_hi, z).
Axes of the slice: x: 4, y: 4 (y_hi: 2, y_lo: 2; y = y_hi * 2 + y_lo), z: 8, core: 2. Of those that a mesh axis runs over, the one named last changes fastest.
Arguments:
- query_tokens: bfloat16 [2, 128, 128, 1536], P(None, 'ha', 'wa'), may hold values from -20 to 20
- key_tokens: bfloat16 [2, 128, 128, 1536], P(None, 'ha', 'wa'), may hold values from -20 to 20
- value_tokens: bfloat16 [2, 128, 128, 1536], P(None, 'ha', 'wa'), may hold values from -6 to 6
- grad_output: bfloat16 [2, 128, 128, 1536], P(None, 'ha', 'wa'), may hold values from -6 to 6
- text_keys: bfloat16 [256, 1536], replicated, may hold values from -6 to 6
- text_values: bfloat16 [256, 1536], replicated, may hold values from -6 to 6
- reach_tiles: int32 [12, 2], replicated, may hold values from 0 to 1, as said below
- text_count: int32 [1], replicated, may hold values from 128 to 256
- pad_mask: int32 [2, 128, 128], replicated, may hold values 0 or 1
Outputs:
- attn_output: bfloat16 [2, 128, 128, 1536], P(None, 'ha', 'wa')
- grad_query: bfloat16 [2, 128, 128, 1536], P(None, 'ha', 'wa')
- grad_key: bfloat16 [2, 128, 128, 1536], P(None, 'ha', 'wa')
- grad_value: bfloat16 [2, 128, 128, 1536], P(None, 'ha', 'wa')
- grad_text_key: bfloat16 [256, 1536], replicated
- grad_text_value: bfloat16 [256, 1536], replicated
Inputs may be any that keep to these rules, and one draw needn't show every extreme that they name: `reach_tiles`: some head has reach 1 along the height tile index and some head reach 0 along the width tile index.
All inputs are finite; a program needn't handle non-finite values.
Results may differ from a plain program's by a relative error of at most 0.025.
Values may be sent and summed in bfloat16 or wider, within the bound.
A program may use at most 128 MiB of HBM per device.

v0:
```python
import jax
import jax.numpy as jnp
from jax import lax
from jax.sharding import PartitionSpec as P

HEADS = 12
HD = 128
TH = 8
TW = 8


def extended(block, sides, width):
    for axis, dim in sides:
        count = lax.axis_size(axis)
        forward = [(i, i + 1) for i in range(count - 1)]
        backward = [(target, source) for source, target in forward]
        low = lax.ppermute(
            lax.slice_in_dim(block, block.shape[dim] - width, None, axis=dim), axis, forward
        )
        high = lax.ppermute(lax.slice_in_dim(block, 0, width, axis=dim), axis, backward)
        block = jnp.concatenate([low, block, high], axis=dim)
    return block


def from_behind(block, axis, distance):
    devices = range(lax.axis_size(axis))
    route = [(i - distance, i) for i in devices if i - distance in devices]
    return lax.ppermute(block, axis, route)


def split_heads(tokens):
    return tokens.reshape(-1, HEADS, HD)


def inner_product(form, left, right):
    return jnp.einsum(form, left, right, preferred_element_type=jnp.float32)


def tile_offsets(frames):
    row_tiles = jnp.arange(3 * TH, dtype=jnp.int32) // TH - 1
    col_tiles = jnp.arange(3 * TW, dtype=jnp.int32) // TW - 1
    row_off = jnp.broadcast_to(row_tiles[None, :, None], (frames, 3 * TH, 3 * TW)).reshape(-1)
    col_off = jnp.broadcast_to(col_tiles[None, None, :], (frames, 3 * TH, 3 * TW)).reshape(-1)
    return (row_off, col_off)


def window(reach_tiles, row_off, col_off):
    return (jnp.abs(row_off)[None, :] <= reach_tiles[:, 0:1]) & (
        jnp.abs(col_off)[None, :] <= reach_tiles[:, 1:2]
    )


def attend(
    query_by_head,
    extended_keys,
    extended_values,
    key_allowed,
    text_key_rows,
    text_value_rows,
    text_allowed,
):
    softmax_scale = HD ** (-0.5)
    video_scores = softmax_scale * inner_product("cfp,qfp->fcq", query_by_head, extended_keys)
    score_text = softmax_scale * inner_product("nhd,jhd->hnj", query_by_head, text_key_rows)
    video_scores = jnp.where(key_allowed[:, None, :], video_scores, -jnp.inf)
    score_text = jnp.where(text_allowed[None, None, :], score_text, -jnp.inf)
    highest = jnp.maximum(jnp.max(video_scores, axis=-1), jnp.max(score_text, axis=-1))
    summed = jnp.sum(jnp.exp(video_scores - highest[..., None]), axis=-1) + jnp.sum(
        jnp.exp(score_text - highest[..., None]), axis=-1
    )
    log_total = highest + jnp.log(summed)
    video_probability = jnp.exp(video_scores - log_total[..., None])
    prob_text = jnp.exp(score_text - log_total[..., None])
    video_rounded_scores = video_probability.astype(jnp.bfloat16)
    text_rounded_scores = prob_text.astype(jnp.bfloat16)
    attention_by_head = (
        inner_product("uzp,pux->zux", video_rounded_scores, extended_values)
        + inner_product("tsm,mtl->stl", text_rounded_scores, text_value_rows)
    ).astype(jnp.bfloat16)
    return (
        attention_by_head,
        log_total,
        video_probability,
        prob_text,
        video_rounded_scores,
        text_rounded_scores,
    )


def body(
    query_tokens,
    key_tokens,
    value_tokens,
    grad_output,
    text_keys,
    text_values,
    reach_tiles,
    text_count,
    pad_mask,
):
    frames = query_tokens.shape[0]
    channels = query_tokens.shape[3]
    softmax_scale = HD ** (-0.5)
    row_index = lax.axis_index("ha")
    col_index = lax.axis_index("wa")
    key_block, value_block = (
        extended(key_tokens, (("ha", 1), ("wa", 2)), TH),
        extended(value_tokens, (("ha", 1), ("wa", 2)), TH),
    )
    query_by_head = split_heads(query_tokens)
    gradient_by_head = split_heads(grad_output)
    extended_keys = split_heads(key_block)
    extended_values = split_heads(value_block)
    text_key_rows = split_heads(text_keys)
    text_value_rows = split_heads(text_values)
    mask_wide = jnp.pad(pad_mask, ((0, 0), (TH, TH), (TW, TW)))
    mask_ext = lax.dynamic_slice(
        mask_wide, (0, row_index * TH, col_index * TW), (frames, 3 * TH, 3 * TW)
    )
    row_off, col_off = tile_offsets(frames)
    inside = window(reach_tiles, row_off, col_off)
    key_allowed = inside & (mask_ext.reshape(-1) > 0)[None, :]
    text_allowed = jnp.arange(text_keys.shape[0], dtype=jnp.int32) < text_count[0]
    (
        attention_by_head,
        log_total,
        video_probability,
        prob_text,
        video_rounded_scores,
        text_rounded_scores,
    ) = attend(
        query_by_head,
        extended_keys,
        extended_values,
        key_allowed,
        text_key_rows,
        text_value_rows,
        text_allowed,
    )
    row_delta_terms = jnp.sum(
        gradient_by_head.astype(jnp.float32) * attention_by_head.astype(jnp.float32), axis=-1
    ).T
    video_slope_terms = (
        video_probability
        * (
            inner_product("cfp,qfp->fcq", gradient_by_head, extended_values)
            - row_delta_terms[..., None]
        )
    ).astype(jnp.bfloat16)
    text_slope_terms = (
        prob_text
        * (
            inner_product("nhd,jhd->hnj", gradient_by_head, text_value_rows)
            - row_delta_terms[..., None]
        )
    ).astype(jnp.bfloat16)
    query_gradient = (
        softmax_scale
        * (
            inner_product("uzp,pux->zux", video_slope_terms, extended_keys)
            + inner_product("tsm,mtl->stl", text_slope_terms, text_key_rows)
        )
    ).astype(jnp.bfloat16)
    text_dk = softmax_scale * inner_product("hnj,nhd->jhd", text_slope_terms, query_by_head)
    text_dv = inner_product("hnj,nhd->jhd", text_rounded_scores, gradient_by_head)
    summed_k, summed_v = lax.psum((text_dk, text_dv), ("ha", "wa"))
    widened_keys = (
        softmax_scale * inner_product("cet,ecj->tcj", video_slope_terms, query_by_head)
    ).reshape(frames, 3 * TH, 3 * TW, channels)
    widened_values = inner_product("cet,ecj->tcj", video_rounded_scores, gradient_by_head).reshape(
        frames, 3 * TH, 3 * TW, channels
    )
    from_east = from_behind((widened_keys[:, :, :TW], widened_values[:, :, :TW]), "wa", -1)
    from_west = from_behind((widened_keys[:, :, 2 * TW :], widened_values[:, :, 2 * TW :]), "wa", 1)
    middle_k = widened_keys[:, :, TW : 2 * TW] + from_east[0] + from_west[0]
    middle_v = widened_values[:, :, TW : 2 * TW] + from_east[1] + from_west[1]
    from_below = from_behind((middle_k[:, :TH], middle_v[:, :TH]), "ha", -1)
    from_above = from_behind((middle_k[:, 2 * TH :], middle_v[:, 2 * TH :]), "ha", 1)
    key_gradient = (middle_k[:, TH : 2 * TH] + from_below[0] + from_above[0]).astype(jnp.bfloat16)
    value_gradient = (middle_v[:, TH : 2 * TH] + from_below[1] + from_above[1]).astype(jnp.bfloat16)
    text_rows = text_keys.shape[0]
    return (
        attention_by_head.reshape(frames, TH, TW, channels),
        query_gradient.reshape(frames, TH, TW, channels),
        key_gradient,
        value_gradient,
        summed_k.reshape(text_rows, channels).astype(jnp.bfloat16),
        summed_v.reshape(text_rows, channels).astype(jnp.bfloat16),
    )


def solution(mesh):
    placed = (
        P(None, "ha", "wa", None),
        P(None, "ha", "wa", None),
        P(None, "ha", "wa", None),
        P(None, "ha", "wa", None),
        P(),
        P(),
        P(),
        P(),
        P(),
    )
    return jax.shard_map(
        body,
        mesh=mesh,
        in_specs=placed,
        out_specs=(
            P(None, "ha", "wa", None),
            P(None, "ha", "wa", None),
            P(None, "ha", "wa", None),
            P(None, "ha", "wa", None),
            P(),
            P(),
        ),
        check_vma=False,
    )
```

profile of v0, /device:TPU:1, one launch (start us, length us, event | category | flops | bytes accessed | tf_op | source)
XLA Modules:
  0.0 419.9 jit_solution(15363276637887954201)
XLA Ops:
  0.7 4.6 %collective-permute-start.4 = (bf16[2,8,8,1536]{3,2,1,0:T(8,128)(2,1)}, bf16[2,8,8,1536]{3,2,1,0:T(8,128)(2,1)}, u32[]{:S(2)}, u32[]{:S(2)}) collective-permute-start(bf16[2,8,8,1536]{3,2,1,0:T(8,128)(2,1)} %param.10), channel_id=1, source_target_pairs={{0,16},{16,32},{32,48},{48,64},{64,80},{80,96},{96,112},{112,128},... | collective-permute-start | bytes 1179656 | tf_op jit(solution)/shard_map/ppermute | solution.py:17
  5.3 2.7 collective-permute-start.5
  8.0 2.9 collective-permute-start
  10.9 2.2 collective-permute-start.1
  13.7 0.8 fusion.35
  14.9 1.3 reshape.180
  16.2 1.3 reshape.184
  17.9 1.2 copy.40
  19.1 1.4 copy.45
  20.5 1.1 constant_dynamic-update-slice_fusion.5
  21.7 1.0 constant_dynamic-update-slice_fusion.3
  22.7 1.3 collective-permute-start.7
  24.0 4.1 collective-permute-start.6
  28.1 1.8 constant_dynamic-update-slice_fusion.2
  29.8 1.8 constant_dynamic-update-slice_fusion.1
  31.6 1.8 constant_dynamic-update-slice_fusion
  33.4 1.3 collective-permute-start.3
  34.7 5.1 %collective-permute-start.2 = (bf16[2,24,8,1536]{3,2,1,0:T(8,128)(2,1)}, bf16[2,24,8,1536]{3,2,1,0:T(8,128)(2,1)}, u32[]{:S(2)}, u32[]{:S(2)}) collective-permute-start(bf16[2,24,8,1536]{3,2,1,0:T(8,128)(2,1)} %constant_dynamic-update-slice_fusion), channel_id=1, source_target_pairs={{0,1},{1,2},{2,3},{3,4},{4,5},{5,6},{6,7},{7,8},{8,9},{9,10},{10,1... | collective-permute-start | bytes 3538952 | tf_op jit(solution)/shard_map/ppermute | solution.py:17
  40.3 12.4 %collective-permute-done.7 = bf16[2,24,8,1536]{3,2,1,0:T(8,128)(2,1)S(1)} collective-permute-done((bf16[2,24,8,1536]{3,2,1,0:T(8,128)(2,1)S(1)}, bf16[2,24,8,1536]{3,2,1,0:T(8,128)(2,1)S(1)}, u32[]{:S(2)}, u32[]{:S(2)}) %collective-permute-start.7) | collective-permute-done | bytes 1179680 | tf_op jit(solution)/shard_map/ppermute | solution.py:20
  52.7 1.0 collective-permute-done.6
  53.6 1.9 pad_maximum_fusion.1
  55.5 7.4 %reshape.179 = bf16[1152,12,128]{2,1,0:T(8,128)(2,1)} reshape(bf16[2,24,24,1536]{3,2,1,0:T(8,128)(2,1)} %pad_maximum_fusion.1) | data formatting | bytes 7077888 | tf_op jit(solution)/shard_map/reshape | solution.py:32
  62.9 6.9 %copy.50 = bf16[1152,12,128]{0,2,1:T(8,128)(2,1)} copy(bf16[1152,12,128]{2,1,0:T(8,128)(2,1)} %reshape.179) | data formatting | bytes 7077888 | tf_op jit(solution)/shard_map/reshape | solution.py:32
  69.8 7.8 %collective-permute-done.3 = bf16[2,24,8,1536]{3,2,1,0:T(8,128)(2,1)} collective-permute-done((bf16[2,24,8,1536]{3,2,1,0:T(8,128)(2,1)}, bf16[2,24,8,1536]{3,2,1,0:T(8,128)(2,1)}, u32[]{:S(2)}, u32[]{:S(2)}) %collective-permute-start.3) | collective-permute-done | bytes 1179680 | tf_op jit(solution)/shard_map/ppermute | solution.py:20
  77.6 1.4 collective-permute-done.2
  79.0 3.3 pad_maximum_fusion
  82.4 7.4 %reshape.178 = bf16[1152,12,128]{2,1,0:T(8,128)(2,1)} reshape(bf16[2,24,24,1536]{3,2,1,0:T(8,128)(2,1)} %pad_maximum_fusion) | data formatting | bytes 7077888 | tf_op jit(solution)/shard_map/reshape | solution.py:32
  89.7 8.4 %bitcast_reduce_fusion = (f32[12,128]{1,0:T(8,128)S(1)}, f32[12,1152,128]{2,1,0:T(8,128)S(1)}) fusion(bf16[1152,12,128]{0,2,1:T(8,128)(2,1)} %copy.50, bf16[128,12,128]{2,1,0:T(8,128)(2,1)S(1)} %reshape.180, pred[12,1152]{1,0:T(8,128)(4,1)S(1)} %and_and_fusion), kind=kOutput, calls=%fused_computation.4 | convolution fusion | flops 458291712 | bytes 11030016 | tf_op jit(solution)/shard_map/cfp,qfp->fcq/dot_general | solution.py:36
  98.7 1.0 fusion.2
  100.2 4.0 convolution_bitcast_fusion
  104.2 3.6 multiply_reduce_fusion
  107.8 2.8 fusion
  110.6 1.1 multiply_bitcast_fusion
  112.5 13.7 %copy.58 = f32[1152,12,128]{2,1,0:T(8,128)} copy(f32[1152,12,128]{2,0,1:T(8,128)S(1)} %multiply_bitcast_fusion) | data formatting | bytes 14155776 | tf_op jit(solution)/shard_map/mul | solution.py:168
  126.2 9.1 %reshape.186 = f32[2,24,24,1536]{3,2,1,0:T(8,128)} reshape(f32[1152,12,128]{2,1,0:T(8,128)} %copy.58) | data formatting | bytes 14155776 | tf_op jit(solution)/shard_map/reshape | solution.py:169
  135.3 4.8 %fusion.39 = (f32[2,24,8,1536]{3,2,1,0:T(8,128)}, f32[2,24,8,1536]{3,2,1,0:T(8,128)}) fusion(f32[2,24,24,1536]{3,2,1,0:T(8,128)} %reshape.186), kind=kLoop, calls=%fused_computation.68 | loop fusion | bytes 9437184 | tf_op jit(solution)/shard_map/slice | solution.py:173
  140.1 1.3 collective-permute-start.8
  141.4 6.1 %collective-permute-start.9 = (f32[2,24,8,1536]{3,2,1,0:T(8,128)}, f32[2,24,8,1536]{3,2,1,0:T(8,128)}, u32[]{:S(2)}, u32[]{:S(2)}) collective-permute-start(f32[2,24,8,1536]{3,2,1,0:T(8,128)} %get-tuple-element.23), channel_id=1, source_target_pairs={{0,1},{1,2},{2,3},{3,4},{4,5},{5,6},{6,7},{7,8},{8,9},{9,10},{10,1... | collective-permute-start | bytes 7077896 | tf_op jit(solution)/shard_map/ppermute | solution.py:28
  147.5 1.8 convolution_bitcast_fusion.1
  149.4 12.7 %copy.60 = f32[1152,12,128]{2,1,0:T(8,128)} copy(f32[1152,12,128]{2,0,1:T(8,128)} %convolution_bitcast_fusion) | data formatting | bytes 14155776 | tf_op jit(solution)/shard_map/cet,ecj->tcj/transpose | solution.py:36
  162.1 9.1 %reshape.187 = f32[2,24,24,1536]{3,2,1,0:T(8,128)} reshape(f32[1152,12,128]{2,1,0:T(8,128)} %copy.60) | data formatting | bytes 14155776 | tf_op jit(solution)/shard_map/reshape | solution.py:170
  171.2 4.9 %fusion.38 = (f32[2,24,8,1536]{3,2,1,0:T(8,128)}, f32[2,24,8,1536]{3,2,1,0:T(8,128)}) fusion(f32[2,24,24,1536]{3,2,1,0:T(8,128)} %reshape.187), kind=kLoop, calls=%fused_computation.67 | loop fusion | bytes 9437184 | tf_op jit(solution)/shard_map/slice | solution.py:173
  176.0 1.4 collective-permute-start.12
  177.5 5.4 %collective-permute-start.13 = (f32[2,24,8,1536]{3,2,1,0:T(8,128)}, f32[2,24,8,1536]{3,2,1,0:T(8,128)}, u32[]{:S(2)}, u32[]{:S(2)}) collective-permute-start(f32[2,24,8,1536]{3,2,1,0:T(8,128)} %get-tuple-element.21), channel_id=1, source_target_pairs={{0,1},{1,2},{2,3},{3,4},{4,5},{5,6},{6,7},{7,8},{8,9},{9,10},{10,1... | collective-permute-start | bytes 7077896 | tf_op jit(solution)/shard_map/ppermute | solution.py:28
  184.3 195.6 %all-reduce.3 = (bf16[256,12,128]{2,0,1:T(8,128)(2,1)}, bf16[256,12,128]{2,0,1:T(8,128)(2,1)}) all-reduce(f32[256,12,128]{2,0,1:T(8,128)S(1)} %multiply_bitcast_fusion.1, f32[256,12,128]{2,0,1:T(8,128)} %convolution_bitcast_fusion.1), channel_id=1, replica_groups=mesh['ha'=16,'wa'=16] {'ha','wa'}, use_global_device_ids=true, to_apply=%region_5.6 | all-reduce | flops 786432 | bytes 4718592 | tf_op jit(solution)/shard_map/psum | solution.py:166
  379.9 3.8 fusion.9
  383.7 1.3 fusion.41
  385.0 4.6 %collective-permute-start.10 = (f32[2,8,8,1536]{3,2,1,0:T(8,128)}, f32[2,8,8,1536]{3,2,1,0:T(8,128)}, u32[]{:S(2)}, u32[]{:S(2)}) collective-permute-start(f32[2,8,8,1536]{3,2,1,0:T(8,128)} %get-tuple-element.26), channel_id=1, source_target_pairs={{16,0},{32,16},{48,32},{64,48},{80,64},{96,80},{112,96},{128,112},... | collective-permute-start | bytes 2359304 | tf_op jit(solution)/shard_map/ppermute | solution.py:28
  389.6 1.9 collective-permute-start.11
  391.5 3.9 fusion.8
  395.5 1.4 copy-done.3
  396.9 1.3 fusion.40
  398.2 3.2 collective-permute-start.14
  401.5 2.8 collective-permute-start.15
  404.3 1.8 fusion.22
  406.1 1.4 copy.56
  407.5 1.0 reshape.185
  409.0 1.0 reshape.183
  410.0 1.4 copy.63
  411.4 1.2 copy.67
  412.6 1.4 copy.66
  414.0 1.2 copy.68
  415.1 2.2 fusion.28
  417.4 2.5 fusion.26
  (56 shorter events, 5.0 us)
Async XLA Ops:
  0.6 17.3 %copy-start.7 = (bf16[256,1536]{1,0:T(8,128)(2,1)S(1)}, bf16[256,1536]{1,0:T(8,128)(2,1)}, u32[]{:S(2)}) copy-start(bf16[256,1536]{1,0:T(8,128)(2,1)} %param.13) | copy-start | bytes 2359300
  0.6 19.8 %copy-start.9 = (s32[12,2]{0,1:T(2,128)S(1)}, s32[12,2]{0,1:T(2,128)}, u32[]{:S(2)}) copy-start(s32[12,2]{0,1:T(2,128)} %param.15) | copy-start | bytes 292
  0.7 19.9 %collective-permute-start.4 = (bf16[2,8,8,1536]{3,2,1,0:T(8,128)(2,1)}, bf16[2,8,8,1536]{3,2,1,0:T(8,128)(2,1)}, u32[]{:S(2)}, u32[]{:S(2)}) collective-permute-start(bf16[2,8,8,1536]{3,2,1,0:T(8,128)(2,1)} %param.10), channel_id=1, source_target_pairs={{0,16},{16,32},{32,48},{48,64},{64,80},{80,96},{96,112},{112,128},... | collective-permute-start | bytes 1179656 | tf_op jit(solution)/shard_map/ppermute | solution.py:17
  5.3 16.4 %collective-permute-start.5 = (bf16[2,8,8,1536]{3,2,1,0:T(8,128)(2,1)}, bf16[2,8,8,1536]{3,2,1,0:T(8,128)(2,1)}, u32[]{:S(2)}, u32[]{:S(2)}) collective-permute-start(bf16[2,8,8,1536]{3,2,1,0:T(8,128)(2,1)} %param.10), channel_id=1, source_target_pairs={{16,0},{32,16},{48,32},{64,48},{80,64},{96,80},{112,96},{128,112},... | collective-permute-start | bytes 1179656 | tf_op jit(solution)/shard_map/ppermute | solution.py:20
  8.0 20.1 %collective-permute-start = (bf16[2,8,8,1536]{3,2,1,0:T(8,128)(2,1)}, bf16[2,8,8,1536]{3,2,1,0:T(8,128)(2,1)}, u32[]{:S(2)}, u32[]{:S(2)}) collective-permute-start(bf16[2,8,8,1536]{3,2,1,0:T(8,128)(2,1)} %param.11), channel_id=1, source_target_pairs={{0,16},{16,32},{32,48},{48,64},{64,80},{80,96},{96,112},{112,128},... | collective-permute-start | bytes 1179656 | tf_op jit(solution)/shard_map/ppermute | solution.py:17
  10.9 20.7 %collective-permute-start.1 = (bf16[2,8,8,1536]{3,2,1,0:T(8,128)(2,1)}, bf16[2,8,8,1536]{3,2,1,0:T(8,128)(2,1)}, u32[]{:S(2)}, u32[]{:S(2)}) collective-permute-start(bf16[2,8,8,1536]{3,2,1,0:T(8,128)(2,1)} %param.11), channel_id=1, source_target_pairs={{16,0},{32,16},{48,32},{64,48},{80,64},{96,80},{112,96},{128,112},... | collective-permute-start | bytes 1179656 | tf_op jit(solution)/shard_map/ppermute | solution.py:20
  17.9 3.7 copy-start.8
  20.5 19.3 %copy-start.4 = (bf16[256,1536]{0,1:T(8,128)(2,1)S(1)}, bf16[256,1536]{0,1:T(8,128)(2,1)}, u32[]{:S(2)}) copy-start(bf16[256,1536]{0,1:T(8,128)(2,1)} %copy.40) | copy-start | bytes 2359300
  22.7 30.0 %collective-permute-start.7 = (bf16[2,24,8,1536]{3,2,1,0:T(8,128)(2,1)S(1)}, bf16[2,24,8,1536]{3,2,1,0:T(8,128)(2,1)S(1)}, u32[]{:S(2)}, u32[]{:S(2)}) collective-permute-start(bf16[2,24,8,1536]{3,2,1,0:T(8,128)(2,1)S(1)} %constant_dynamic-update-slice_fusion.3), channel_id=1, source_target_pairs={{1,0},{2,1},{3,2},{4,3},{5,4},{6,5},{7,6},{8,7},{9,8},{10,9},{11,1... | collective-permute-start | bytes 3538952 | tf_op jit(solution)/shard_map/ppermute | solution.py:20
  24.0 29.7 %collective-permute-start.6 = (bf16[2,24,8,1536]{3,2,1,0:T(8,128)(2,1)S(1)}, bf16[2,24,8,1536]{3,2,1,0:T(8,128)(2,1)S(1)}, u32[]{:S(2)}, u32[]{:S(2)}) collective-permute-start(bf16[2,24,8,1536]{3,2,1,0:T(8,128)(2,1)S(1)} %constant_dynamic-update-slice_fusion.3), channel_id=1, source_target_pairs={{0,1},{1,2},{2,3},{3,4},{4,5},{5,6},{6,7},{7,8},{8,9},{9,10},{10,1... | collective-permute-start | bytes 3538952 | tf_op jit(solution)/shard_map/ppermute | solution.py:17
  33.4 44.2 %collective-permute-start.3 = (bf16[2,24,8,1536]{3,2,1,0:T(8,128)(2,1)}, bf16[2,24,8,1536]{3,2,1,0:T(8,128)(2,1)}, u32[]{:S(2)}, u32[]{:S(2)}) collective-permute-start(bf16[2,24,8,1536]{3,2,1,0:T(8,128)(2,1)} %constant_dynamic-update-slice_fusion), channel_id=1, source_target_pairs={{1,0},{2,1},{3,2},{4,3},{5,4},{6,5},{7,6},{8,7},{9,8},{10,9},{11,1... | collective-permute-start | bytes 3538952 | tf_op jit(solution)/shard_map/ppermute | solution.py:20
  34.7 44.4 %collective-permute-start.2 = (bf16[2,24,8,1536]{3,2,1,0:T(8,128)(2,1)}, bf16[2,24,8,1536]{3,2,1,0:T(8,128)(2,1)}, u32[]{:S(2)}, u32[]{:S(2)}) collective-permute-start(bf16[2,24,8,1536]{3,2,1,0:T(8,128)(2,1)} %constant_dynamic-update-slice_fusion), channel_id=1, source_target_pairs={{0,1},{1,2},{2,3},{3,4},{4,5},{5,6},{6,7},{7,8},{8,9},{9,10},{10,1... | collective-permute-start | bytes 3538952 | tf_op jit(solution)/shard_map/ppermute | solution.py:17
  99.7 4.5 %slice-start = ((s8[4718592]{0:T(1024)(128)(4,1)}), s8[4194304]{0:T(1024)(128)(4,1)S(1)}, s32[]{:S(2)}) async-start(s8[4718592]{0:T(1024)(128)(4,1)} %bitcast.81), calls=%async_computation | async-start | bytes 8388608
  100.2 4.0 slice-start.1
  110.6 1.9 copy-start.1
  140.1 239.8 %collective-permute-start.8 = (f32[2,24,8,1536]{3,2,1,0:T(8,128)}, f32[2,24,8,1536]{3,2,1,0:T(8,128)}, u32[]{:S(2)}, u32[]{:S(2)}) collective-permute-start(f32[2,24,8,1536]{3,2,1,0:T(8,128)} %get-tuple-element.22), channel_id=1, source_target_pairs={{1,0},{2,1},{3,2},{4,3},{5,4},{6,5},{7,6},{8,7},{9,8},{10,9},{11,1... | collective-permute-start | bytes 7077896 | tf_op jit(solution)/shard_map/ppermute | solution.py:28
  141.4 238.5 %collective-permute-start.9 = (f32[2,24,8,1536]{3,2,1,0:T(8,128)}, f32[2,24,8,1536]{3,2,1,0:T(8,128)}, u32[]{:S(2)}, u32[]{:S(2)}) collective-permute-start(f32[2,24,8,1536]{3,2,1,0:T(8,128)} %get-tuple-element.23), channel_id=1, source_target_pairs={{0,1},{1,2},{2,3},{3,4},{4,5},{5,6},{6,7},{7,8},{8,9},{9,10},{10,1... | collective-permute-start | bytes 7077896 | tf_op jit(solution)/shard_map/ppermute | solution.py:28
  176.0 7.9 %copy-start.5 = (bf16[256,1536]{0,1:T(8,128)(2,1)S(1)}, bf16[256,1536]{0,1:T(8,128)(2,1)}, u32[]{:S(2)}) copy-start(bf16[256,1536]{0,1:T(8,128)(2,1)} %copy.40) | copy-start | bytes 2359300
  176.0 215.5 %collective-permute-start.12 = (f32[2,24,8,1536]{3,2,1,0:T(8,128)}, f32[2,24,8,1536]{3,2,1,0:T(8,128)}, u32[]{:S(2)}, u32[]{:S(2)}) collective-permute-start(f32[2,24,8,1536]{3,2,1,0:T(8,128)} %get-tuple-element.20), channel_id=1, source_target_pairs={{1,0},{2,1},{3,2},{4,3},{5,4},{6,5},{7,6},{8,7},{9,8},{10,9},{11,1... | collective-permute-start | bytes 7077896 | tf_op jit(solution)/shard_map/ppermute | solution.py:28
  177.5 214.1 %collective-permute-start.13 = (f32[2,24,8,1536]{3,2,1,0:T(8,128)}, f32[2,24,8,1536]{3,2,1,0:T(8,128)}, u32[]{:S(2)}, u32[]{:S(2)}) collective-permute-start(f32[2,24,8,1536]{3,2,1,0:T(8,128)} %get-tuple-element.21), channel_id=1, source_target_pairs={{0,1},{1,2},{2,3},{3,4},{4,5},{5,6},{6,7},{7,8},{8,9},{9,10},{10,1... | collective-permute-start | bytes 7077896 | tf_op jit(solution)/shard_map/ppermute | solution.py:28
  385.0 30.1 %collective-permute-start.10 = (f32[2,8,8,1536]{3,2,1,0:T(8,128)}, f32[2,8,8,1536]{3,2,1,0:T(8,128)}, u32[]{:S(2)}, u32[]{:S(2)}) collective-permute-start(f32[2,8,8,1536]{3,2,1,0:T(8,128)} %get-tuple-element.26), channel_id=1, source_target_pairs={{16,0},{32,16},{48,32},{64,48},{80,64},{96,80},{112,96},{128,112},... | collective-permute-start | bytes 2359304 | tf_op jit(solution)/shard_map/ppermute | solution.py:28
  389.6 25.6 %collective-permute-start.11 = (f32[2,8,8,1536]{3,2,1,0:T(8,128)}, f32[2,8,8,1536]{3,2,1,0:T(8,128)}, u32[]{:S(2)}, u32[]{:S(2)}) collective-permute-start(f32[2,8,8,1536]{3,2,1,0:T(8,128)} %get-tuple-element.27), channel_id=1, source_target_pairs={{0,16},{16,32},{32,48},{48,64},{64,80},{80,96},{96,112},{112,128},... | collective-permute-start | bytes 2359304 | tf_op jit(solution)/shard_map/ppermute | solution.py:28
  391.5 12.7 %copy-start = (bf16[1152,12,128]{0,2,1:T(8,128)(2,1)S(1)}, bf16[1152,12,128]{0,2,1:T(8,128)(2,1)}, u32[]{:S(2)}) copy-start(bf16[1152,12,128]{0,2,1:T(8,128)(2,1)} %copy.50) | copy-start | bytes 10616836
  391.5 12.7 %copy-start.2 = (bf16[12,128,1152]{1,2,0:T(8,128)(2,1)S(1)}, bf16[12,128,1152]{1,2,0:T(8,128)(2,1)}, u32[]{:S(2)}) copy-start(bf16[12,128,1152]{1,2,0:T(8,128)(2,1)} %copy-done.1) | copy-start | bytes 10616836
  395.5 1.4 copy-start.3
  398.2 19.2 %collective-permute-start.14 = (f32[2,8,8,1536]{3,2,1,0:T(8,128)}, f32[2,8,8,1536]{3,2,1,0:T(8,128)}, u32[]{:S(2)}, u32[]{:S(2)}) collective-permute-start(f32[2,8,8,1536]{3,2,1,0:T(8,128)} %get-tuple-element.24), channel_id=1, source_target_pairs={{16,0},{32,16},{48,32},{64,48},{80,64},{96,80},{112,96},{128,112},... | collective-permute-start | bytes 2359304 | tf_op jit(solution)/shard_map/ppermute | solution.py:28
  401.5 7.1 %copy-start.6 = (bf16[128,12,128]{0,2,1:T(8,128)(2,1)S(1)}, bf16[128,12,128]{0,2,1:T(8,128)(2,1)}, u32[]{:S(2)}) copy-start(bf16[128,12,128]{0,2,1:T(8,128)(2,1)} %get-tuple-element.35) | copy-start | bytes 1179652
  401.5 15.9 %collective-permute-start.15 = (f32[2,8,8,1536]{3,2,1,0:T(8,128)}, f32[2,8,8,1536]{3,2,1,0:T(8,128)}, u32[]{:S(2)}, u32[]{:S(2)}) collective-permute-start(f32[2,8,8,1536]{3,2,1,0:T(8,128)} %get-tuple-element.25), channel_id=1, source_target_pairs={{0,16},{16,32},{32,48},{48,64},{64,80},{80,96},{96,112},{112,128},... | collective-permute-start | bytes 2359304 | tf_op jit(solution)/shard_map/ppermute | solution.py:28
where the time goes:
time: 426 us; the launch traced here: 420 us
  blocking collectives  196 us (46%)
  local copies, waits for them, and re-layouts  103 us (24%)
  starting transfers between devices  50.8 us (12%)
  matrix products  25.9 us (6%)
  waiting for transfers between devices  22.6 us (5%)
  other arithmetic  20.1 us (5%)
    psum x1, blocking collectives, body(): summed_k, summed_v = lax.psum((text_dk, text_dv), ('ha', 'wa'))  196 us
    ppermute x8, starting transfers between devices, from_behind(): return lax.ppermute(block, axis, route)  26.7 us
    dot_general x12, matrix products, inner_product(): return jnp.einsum(form, left, right, preferred_element_type=jnp.float32)  25.9 us
    reshape x6, local copies, waits for them, and re-layouts, split_heads(): return tokens.reshape(-1, HEADS, HD)  24.6 us
    ppermute x4, waiting for transfers between devices, extended(): lax.ppermute(lax.slice_in_dim(block, 0, width, axis=dim), axis, backward)  20.2 us
    ppermute x4, starting transfers between devices, extended(): lax.ppermute(lax.slice_in_dim(block, block.shape[dim] - width, None, axis...  16.7 us
    mul x1, local copies, waits for them, and re-layouts, body(): softmax_scale * inner_product('cet,ecj->tcj', video_slope_terms, query_by...  13.7 us
    transpose x1, local copies, waits for them, and re-layouts, inner_product(): return jnp.einsum(form, left, right, preferred_element_type=jnp.float32)  12.7 us
  transfers between devices with their start and end apart: 16, of which 4 were waited for; matrix products, arithmetic and copies ran while one was open for 20% of the time, Pallas kernels for 0%

commit v1 on v0

v1 whole, which is shorter than its diff:
```python
import functools
import math

import jax
import jax.numpy as jnp
from jax import lax
from jax.experimental import pallas as pl
from jax.experimental.pallas import tpu as pltpu
from jax.sharding import PartitionSpec as P

HEADS = 12
HD = 128
TH = 8
TW = 8
TOK = 128
TEXT = 256
VID = 9 * TOK
KEYS = VID + TEXT
CH = HEADS * HD
GROUPS = 3
PER = HEADS // GROUPS
ROWS = TEXT // 8
SCALE = HD**-0.5
SCALE2 = SCALE * math.log2(math.e)
BIG = 1e30
MESH = pl.DeviceIdType.MESH
F32 = jnp.float32
BF16 = jnp.bfloat16
OFFSETS = tuple((dr, dc) for dr in (-1, 0, 1) for dc in (-1, 0, 1))


def dot_nt(a, b):
    return lax.dot_general(a, b, (((1,), (1,)), ((), ())), preferred_element_type=F32)


def dot_nn(a, b):
    return lax.dot_general(a, b, (((1,), (0,)), ((), ())), preferred_element_type=F32)


def dot_tn(a, b):
    return lax.dot_general(a, b, (((0,), (0,)), ((), ())), preferred_element_type=F32)


def cols(head):
    return pl.ds(pl.multiple_of(head * HD, HD), HD)


class Copy:
    def __init__(self, sems, number, src, dst, device, sends=None, receives=None):
        self.copy = pltpu.make_async_remote_copy(
            src_ref=src,
            dst_ref=dst,
            send_sem=sems[0].at[number],
            recv_sem=sems[1].at[number],
            device_id=device,
            device_id_type=MESH,
        )
        self.sends = sends
        self.receives = receives

    def start(self):
        if self.sends is None:
            self.copy.start()
        else:
            pl.when(self.sends)(self.copy.start)

    def wait_recv(self):
        if self.receives is None:
            self.copy.wait_recv()
        else:
            pl.when(self.receives)(self.copy.wait_recv)

    def wait_send(self):
        if self.sends is None:
            self.copy.wait_send()
        else:
            pl.when(self.sends)(self.copy.wait_send)


def main_kernel(
    sizes,
    q_ref,
    k_ref,
    v_ref,
    d_ref,
    tk_ref,
    tv_ref,
    bias_ref,
    qbias_ref,
    pad_ref,
    attn_ref,
    gq_ref,
    gk_ref,
    gv_ref,
    text_ref,
    kv_sw,
    kv_sh,
    kv_sc,
    kv_rw,
    kv_rh,
    kv_rc,
    qd_sw,
    qd_sh,
    qd_sc,
    qd_rw,
    qd_rh,
    qd_rc,
    left_ext,
    right_ext,
    stat_acc,
    stat_ext,
    own_part,
    pair_src,
    pair_dst,
    a_src,
    a_dst,
    z_acc,
    z_src,
    z_dst,
    b_all,
    send_sems,
    recv_sems,
):
    m_w, m_h, m_c = sizes
    ha = lax.axis_index("ha")
    wa = lax.axis_index("wa")
    core = ha % 2
    x = (ha // 2) % 4
    y = (wa // 8) * 2 + ha // 8
    z = wa % 8

    def device(y_, x_, core_, z_):
        return ((y_ % 2) * 8 + x_ * 2 + core_, (y_ // 2) * 8 + z_)

    def a_partner(step):
        along = (core * x + (1 - core) * y + step) % 4
        return along, device(core * y + (1 - core) * along, core * along + (1 - core) * x, core, z)

    def b_partner(step):
        along = (core * y + (1 - core) * x + step) % 4
        return along, device(core * along + (1 - core) * y, core * x + (1 - core) * along, core, z)

    def z_partner(step):
        along = (z + step) % 8
        return along, device(y, x, core, along)

    a_me = core * x + (1 - core) * y
    b_me = core * y + (1 - core) * x
    pair = device(y, x, 1 - core, z)
    has = {-1: (ha > 0, wa > 0), 1: (ha < 15, wa < 15)}

    def exists(dr, dc):
        terms = [has[dr][0]] if dr else []
        terms += [has[dc][1]] if dc else []
        return functools.reduce(jnp.logical_and, terms)

    barrier = pltpu.get_barrier_semaphore()

    def greet(target):
        pl.semaphore_signal(barrier, inc=1, device_id=target, device_id_type=MESH)

    expected = jnp.int32(14)
    for dr, dc in OFFSETS:
        if dr or dc:
            there = exists(dr, dc)
            pl.when(there)(functools.partial(greet, (ha + dr, wa + dc)))
            expected = expected + there.astype(jnp.int32)
    for step in (1, 2, 3):
        greet(a_partner(step)[1])
        greet(b_partner(step)[1])
    for step in range(1, 8):
        greet(z_partner(step)[1])
    greet(pair)

    counter = [0]
    sems = (send_sems, recv_sems)

    def copy(src, dst, target, sends=None, receives=None):
        number = counter[0]
        counter[0] += 1
        return Copy(sems, number, src, dst, target, sends, receives)

    def pack(first, second, sw, sh):
        for index, ref in ((0, first), (1, second)):
            for i in range(m_w):
                sw[index * m_w + i] = ref[:, cols(i)]
            for i in range(m_h):
                sh[index * m_h + i] = ref[:, cols(i)]

    def pack_corners(rw, sc):
        for side in (0, 1):
            for index in (0, 1):
                for i in range(m_c):
                    sc[side, index * m_c + i] = rw[side, index * m_w + i]

    def blank(rw, rh, rc):
        for side, sign in ((0, -1), (1, 1)):

            @pl.when(jnp.logical_not(has[sign][1]))
            def _():
                rw[side] = jnp.zeros(rw.shape[1:], rw.dtype)

            @pl.when(jnp.logical_not(has[sign][0]))
            def _():
                rh[side] = jnp.zeros(rh.shape[1:], rh.dtype)
                rc[side] = jnp.zeros(rc.shape[1:], rc.dtype)

    def halo(sw, sh, sc, rw, rh, rc):
        along_w, along_h, corner = [], [], []
        for side, sign in ((0, 1), (1, -1)):
            to, source = has[sign], has[-sign]
            along_w.append(copy(sw, rw.at[side], (ha, wa + sign), to[1], source[1]))
            along_h.append(copy(sh, rh.at[side], (ha + sign, wa), to[0], source[0]))
            corner.append(copy(sc, rc.at[side], (ha + sign, wa), to[0], source[0]))
        return along_w, along_h, corner

    kv_w, kv_h, kv_c = halo(kv_sw, kv_sh, kv_sc, kv_rw, kv_rh, kv_rc)
    qd_w, qd_h, qd_c = halo(qd_sw, qd_sh, qd_sc, qd_rw, qd_rh, qd_rc)
    stat_copies = [
        copy(
            stat_ext.at[4],
            stat_ext.at[(1 - dr) * 3 + (1 - dc)],
            (ha + dr, wa + dc),
            exists(dr, dc),
            exists(-dr, -dc),
        )
        for dr, dc in OFFSETS
        if dr or dc
    ]

    pack(k_ref, v_ref, kv_sw, kv_sh)
    pl.semaphore_wait(barrier, expected)
    for c in kv_w + kv_h:
        c.start()
    pack(q_ref, d_ref, qd_sw, qd_sh)
    blank(kv_rw, kv_rh, kv_rc)
    blank(qd_rw, qd_rh, qd_rc)
    for dr, dc in OFFSETS:
        if dr or dc:

            @pl.when(jnp.logical_not(exists(dr, dc)))
            def _():
                stat_ext[(dr + 1) * 3 + dc + 1] = jnp.zeros((32, TOK), F32)

    def assemble(ext, own_ref, index, rw, rh, rc, head):
        w, h, c = head, head, head
        for tile, (dr, dc) in enumerate(OFFSETS):
            if dr == 0 and dc == 0:
                block = own_ref[:, cols(head)]
            elif dr == 0:
                block = rw[(dc + 1) // 2, index * m_w + w]
            elif dc == 0:
                block = rh[(dr + 1) // 2, index * m_h + h]
            else:
                block = rc[(dr + 1) // 2, (dc + 1) // 2, index * m_c + c]
            ext[pl.ds(tile * TOK, TOK), :] = block

    lane = lax.broadcasted_iota(jnp.int32, (TOK, TOK), 1)

    def own_pass(head):
        assemble(left_ext, k_ref, 0, kv_rw, kv_rh, kv_rc, head)
        assemble(right_ext, v_ref, 1, kv_rw, kv_rh, kv_rc, head)
        left_ext[pl.ds(VID, TEXT), :] = tk_ref[:, cols(head)]
        right_ext[pl.ds(VID, TEXT), :] = tv_ref[:, cols(head)]
        query, grad = q_ref[:, cols(head)], d_ref[:, cols(head)]
        scores = dot_nt(query, left_ext[...]) * SCALE2 + bias_ref[pl.ds(head, 1), :]
        highest = jnp.max(scores, axis=1, keepdims=True)
        powers = jnp.exp2(scores - highest)
        total = jnp.sum(powers, axis=1, keepdims=True)
        probs = powers * (1.0 / total)
        probs_b = probs.astype(BF16)
        attn = dot_nn(probs_b, right_ext[...]).astype(BF16)
        attn_ref[:, cols(head)] = attn
        delta = jnp.sum(grad.astype(F32) * attn.astype(F32), axis=1, keepdims=True)
        slopes = (probs * (dot_nt(grad, right_ext[...]) - delta)).astype(BF16)
        gq_ref[:, cols(head)] = (SCALE * dot_nn(slopes, left_ext[...])).astype(BF16)
        log_total = highest + jnp.log(total) * math.log2(math.e)
        stat_acc[...] = jnp.where(
            lane == head, log_total, jnp.where(lane == head + 16, delta, stat_acc[...])
        )
        text_k = SCALE * dot_tn(slopes[:, VID:], query)
        text_v = dot_tn(probs_b[:, VID:], grad)
        own_part[head] = jnp.where(core == 0, text_k, text_v)
        pair_src[head] = jnp.where(core == 0, text_v, text_k).astype(BF16)

    def owner_pass(head):
        assemble(left_ext, q_ref, 0, qd_rw, qd_rh, qd_rc, head)
        assemble(right_ext, d_ref, 1, qd_rw, qd_rh, qd_rc, head)
        log_total = jnp.concatenate([stat_ext[t, pl.ds(head, 1), :] for t in range(9)], axis=1)
        delta = jnp.concatenate([stat_ext[t, pl.ds(head + 16, 1), :] for t in range(9)], axis=1)
        shift = log_total + qbias_ref[pl.ds(head, 1), :]
        queries, grads = left_ext[pl.ds(0, VID), :], right_ext[pl.ds(0, VID), :]
        probs = jnp.exp2(dot_nt(k_ref[:, cols(head)], queries) * SCALE2 - shift)
        slopes = (probs * (dot_nt(v_ref[:, cols(head)], grads) - delta)).astype(BF16)
        real = pad_ref[...] > 0
        gk_ref[:, cols(head)] = jnp.where(real, SCALE * dot_nn(slopes, queries), 0.0).astype(BF16)
        gv_ref[:, cols(head)] = jnp.where(real, dot_nn(probs.astype(BF16), grads), 0.0).astype(BF16)

    started = []

    def stage_pair(g):
        span = pl.ds(g * PER, PER)
        made = [copy(pair_src.at[span], pair_dst.at[span], pair)]
        return made, None

    def prepare_a(g):
        for i in range(PER):
            own_part[g * PER + i] = own_part[g * PER + i] + pair_dst[g * PER + i].astype(F32)

        made = []
        for step in (1, 2, 3):
            along, target = a_partner(step)
            a_src[g, step - 1] = own_part[g * PER + along].astype(BF16)
            made.append(copy(a_src.at[g, step - 1], a_dst.at[g, step - 1], target))
        return made

    def prepare_z(g):
        z_acc[g] = (
            own_part[g * PER + a_me]
            + a_dst[g, 0].astype(F32)
            + a_dst[g, 1].astype(F32)
            + a_dst[g, 2].astype(F32)
        )
        z_src[g] = z_acc[g].astype(BF16)
        made = []
        for step in range(1, 8):
            along, target = z_partner(step)
            rows = pl.ds(pl.multiple_of(along * ROWS, ROWS), ROWS)
            made.append(copy(z_src.at[g, rows], z_dst.at[g, step - 1], target))
        return made

    def prepare_b(g):
        total = z_acc[g, pl.ds(pl.multiple_of(z * ROWS, ROWS), ROWS), :]
        for step in range(7):
            total = total + z_dst[g, step].astype(F32)
        b_all[g, b_me] = total.astype(BF16)
        return [
            copy(b_all.at[g, b_me], b_all.at[g, b_me], b_partner(step)[1]) for step in (1, 2, 3)
        ]

    def prepare_z_back(g):
        total = b_all[g, 0].astype(F32)
        for i in (1, 2, 3):
            total = total + b_all[g, i].astype(F32)
        rows = pl.ds(pl.multiple_of(z * ROWS, ROWS), ROWS)
        piece = text_ref.at[core, g * PER + a_me, rows]
        text_ref[core, g * PER + a_me, rows, :] = total.astype(BF16)
        return [copy(piece, piece, z_partner(step)[1]) for step in range(1, 8)]

    def prepare_a_back(g):
        piece = text_ref.at[core, g * PER + a_me]
        return [copy(piece, piece, a_partner(step)[1]) for step in (1, 2, 3)]

    def prepare_pair_back(g):
        piece = text_ref.at[core, pl.ds(g * PER, PER)]
        return [copy(piece, piece, pair)]

    stages = (
        lambda g: stage_pair(g)[0],
        prepare_a,
        prepare_z,
        prepare_b,
        prepare_z_back,
        prepare_a_back,
        prepare_pair_back,
        lambda g: [],
    )
    flying = [[] for _ in range(GROUPS)]
    level = [0] * GROUPS

    def advance(g):
        if level[g] >= len(stages):
            return
        for c in flying[g]:
            c.wait_recv()
        flying[g] = stages[level[g]](g)
        level[g] += 1
        for c in flying[g]:
            c.start()
        started.extend(flying[g])

    for c in kv_w:
        c.wait_recv()
    pack_corners(kv_rw, kv_sc)
    for c in kv_c + qd_w + qd_h:
        c.start()
    for c in kv_h + kv_c:
        c.wait_recv()

    stat_acc[...] = jnp.zeros((TOK, TOK), F32)
    for g in range(GROUPS):

        @pl.loop(g * PER, (g + 1) * PER)
        def _(head):
            own_pass(head)

        if g == GROUPS - 1:
            stat_ext[4] = jnp.transpose(stat_acc[...])[:32]
            for c in stat_copies:
                c.start()
        for earlier in range(g + 1):
            advance(earlier)
        if g == 0:
            for c in qd_w:
                c.wait_recv()
            pack_corners(qd_rw, qd_sc)
            for c in qd_c:
                c.start()

    for c in qd_h + qd_c + stat_copies:
        c.wait_recv()
    for part in range(6):
        for g in range(GROUPS):
            advance(g)

        @pl.loop(part * 2, part * 2 + 2)
        def _(head):
            owner_pass(head)

    for _ in stages:
        for g in range(GROUPS):
            advance(g)
    for c in kv_w + kv_h + kv_c + qd_w + qd_h + qd_c + stat_copies + started:
        c.wait_send()
    assert counter[0] == N_COPIES


N_COPIES = 20 + GROUPS * 25


def finish_kernel(attn, gq, gk, gv, text, o_attn, o_gq, o_gk, o_gv, o_tk, o_tv, sems):
    moves = [
        pltpu.make_async_copy(s, d, sems.at[i])
        for i, (s, d) in enumerate(((attn, o_attn), (gq, o_gq), (gk, o_gk), (gv, o_gv)))
    ]
    for side, out in ((0, o_tk), (1, o_tv)):
        for h in range(HEADS):
            moves.append(
                pltpu.make_async_copy(
                    text.at[side, h],
                    out.at[:, pl.ds(h * HD, HD)],
                    sems.at[4 + side * HEADS + h],
                )
            )
    for m in moves:
        m.start()
    for m in moves:
        m.wait()


def fused(sizes, operands):
    m_w, m_h, m_c = sizes
    vmem = pl.BlockSpec(memory_space=pltpu.VMEM)
    halo = [
        pltpu.VMEM((2 * m_w, TOK, HD), BF16),
        pltpu.VMEM((2 * m_h, TOK, HD), BF16),
        pltpu.VMEM((2, 2 * m_c, TOK, HD), BF16),
        pltpu.VMEM((2, 2 * m_w, TOK, HD), BF16),
        pltpu.VMEM((2, 2 * m_h, TOK, HD), BF16),
        pltpu.VMEM((2, 2, 2 * m_c, TOK, HD), BF16),
    ]
    token = jax.ShapeDtypeStruct((TOK, CH), BF16)
    return pl.pallas_call(
        functools.partial(main_kernel, sizes),
        out_shape=(
            token,
            token,
            token,
            token,
            jax.ShapeDtypeStruct((2, HEADS, TEXT, HD), BF16),
        ),
        in_specs=[vmem] * 9,
        out_specs=(vmem,) * 5,
        scratch_shapes=halo
        + halo
        + [
            pltpu.VMEM((KEYS, HD), BF16),
            pltpu.VMEM((KEYS, HD), BF16),
            pltpu.VMEM((TOK, TOK), F32),
            pltpu.VMEM((9, 32, TOK), F32),
            pltpu.VMEM((HEADS, TEXT, HD), F32),
            pltpu.VMEM((HEADS, TEXT, HD), BF16),
            pltpu.VMEM((HEADS, TEXT, HD), BF16),
            pltpu.VMEM((GROUPS, 3, TEXT, HD), BF16),
            pltpu.VMEM((GROUPS, 3, TEXT, HD), BF16),
            pltpu.VMEM((GROUPS, TEXT, HD), F32),
            pltpu.VMEM((GROUPS, TEXT, HD), BF16),
            pltpu.VMEM((GROUPS, 7, ROWS, HD), BF16),
            pltpu.VMEM((GROUPS, 4, ROWS, HD), BF16),
            pltpu.SemaphoreType.DMA((N_COPIES,)),
            pltpu.SemaphoreType.DMA((N_COPIES,)),
        ],
        compiler_params=pltpu.CompilerParams(
            collective_id=0, has_side_effects=True, vmem_limit_bytes=56 * 1024 * 1024
        ),
    )(*operands)


def finish(attn, gq, gk, gv, text):
    any_space = pl.BlockSpec(memory_space=pl.ANY)
    token = jax.ShapeDtypeStruct((TOK, CH), BF16)
    rows = jax.ShapeDtypeStruct((TEXT, CH), BF16)
    return pl.pallas_call(
        finish_kernel,
        out_shape=(token, token, token, token, rows, rows),
        in_specs=[any_space] * 5,
        out_specs=(any_space,) * 6,
        scratch_shapes=[pltpu.SemaphoreType.DMA((4 + 2 * HEADS,))],
    )(attn, gq, gk, gv, text)


def body(
    query_tokens,
    key_tokens,
    value_tokens,
    grad_output,
    text_keys,
    text_values,
    reach_tiles,
    text_count,
    pad_mask,
):
    frames = query_tokens.shape[0]
    ha = lax.axis_index("ha")
    wa = lax.axis_index("wa")
    dr = jnp.array([o[0] for o in OFFSETS], jnp.int32)
    dc = jnp.array([o[1] for o in OFFSETS], jnp.int32)
    inside = (jnp.abs(dr)[None] <= reach_tiles[:, 0:1]) & (jnp.abs(dc)[None] <= reach_tiles[:, 1:2])
    wide = jnp.pad(pad_mask, ((0, 0), (TH, TH), (TW, TW)))
    tiles = lax.dynamic_slice(wide, (0, ha * TH, wa * TW), (frames, 3 * TH, 3 * TW))
    tiles = tiles.reshape(frames, 3, TH, 3, TW).transpose(1, 3, 0, 2, 4).reshape(9, TOK)
    allowed = inside[:, :, None] & (tiles > 0)[None]
    live = jnp.broadcast_to(jnp.arange(TEXT, dtype=jnp.int32) < text_count[0], (HEADS, TEXT))
    bias = jnp.where(
        jnp.concatenate([allowed.reshape(HEADS, VID), live], axis=1), 0.0, -BIG
    ).astype(F32)
    there = (ha + dr >= 0) & (ha + dr < 16) & (wa + dc >= 0) & (wa + dc < 16)
    qbias = jnp.where(inside & there[None], 0.0, BIG).astype(F32)
    qbias = jnp.broadcast_to(qbias[:, :, None], (HEADS, 9, TOK)).reshape(HEADS, VID)
    pad = jnp.broadcast_to(tiles[4][:, None], (TOK, HD)).astype(F32)
    operands = [t.reshape(TOK, CH) for t in (query_tokens, key_tokens, value_tokens, grad_output)]
    operands += [text_keys, text_values, bias, qbias, pad]
    attn, gq, gk, gv, tk, tv = finish(*fused((HEADS, HEADS, HEADS), operands))
    shape = query_tokens.shape
    return (
        attn.reshape(shape),
        gq.reshape(shape),
        gk.reshape(shape),
        gv.reshape(shape),
        tk,
        tv,
    )


def solution(mesh):
    tokens = P(None, "ha", "wa", None)
    return jax.shard_map(
        body,
        mesh=mesh,
        in_specs=(tokens,) * 4 + (P(),) * 5,
        out_specs=(tokens,) * 4 + (P(), P()),
        check_vma=False,
    )
```

time: 426 us -> 239 us (0.56); the launches traced: 420 us -> 239 us
  Pallas kernels: 0 us -> 231 us
  blocking collectives: 196 us -> 0 us
  local copies, waits for them, and re-layouts: 103 us -> 3.49 us
  starting transfers between devices: 50.8 us -> 0 us
  matrix products: 25.9 us -> 0 us
  waiting for transfers between devices: 22.6 us -> 0 us
  other arithmetic: 20.1 us -> 2.88 us
    pallas_call x0 -> x2, Pallas kernels: none -> 231 us  [the longest x1 134 us: fused(): pl.pallas_call(functools.partial(main_kernel, sizes), out_shape=(token, t...]
    psum x1 -> x0, blocking collectives: 196 us -> none  [body(): summed_k, summed_v = lax.psum((text_dk, text_dv), ('ha', 'wa'))]
    ppermute x16 -> x0, starting transfers between devices: 50.8 us -> none  [the longest x8 26.7 us: from_behind(): return lax.ppermute(block, axis, route)]
    reshape x10 -> x2, local copies, waits for them, and re-layouts: 44.8 us -> 0.2 us  [body(): tiles.reshape(frames, 3, TH, 3, TW).transpose(1, 3, 0, 2, 4).reshape(9, TOK)]
    dot_general x12 -> x0, matrix products: 25.9 us -> none  [inner_product(): return jnp.einsum(form, left, right, preferred_element_type=jnp.float32)]
    ppermute x16 -> x0, waiting for transfers between devices: 22.6 us -> none  [the longest x4 20.2 us: extended(): lax.ppermute(lax.slice_in_dim(block, 0, width, axis=dim), axis, backward)]
    mul x1 -> x0, local copies, waits for them, and re-layouts: 13.7 us -> none  [body(): softmax_scale * inner_product('cet,ecj->tcj', video_slope_terms, query_by...]
    transpose x1 -> x0, local copies, waits for them, and re-layouts: 12.7 us -> none  [inner_product(): return jnp.einsum(form, left, right, preferred_element_type=jnp.float32)]
  transfers between devices with their start and end apart: 16 -> 0, of which waited for: 4 -> 0; matrix products, arithmetic and copies ran while one was open for 20% -> 0% of each run, Pallas kernels for 0% -> 0%
where the time goes in v1:
time: 239 us
  Pallas kernels  231 us (97%)
  local copies, waits for them, and re-layouts  3.49 us (1%)
  other arithmetic  2.88 us (1%)
    pallas_call x1, Pallas kernels, fused(): pl.pallas_call(functools.partial(main_kernel, sizes), out_shape=(token, t...  134 us
    pallas_call x1, Pallas kernels, finish(): pl.pallas_call(finish_kernel, out_shape=(token, token, token, token, rows...  96.6 us

profile of v1, /device:TPU:1, one launch (start us, length us, event | category | flops | bytes accessed | tf_op | source)
XLA Modules:
  0.0 238.6 jit_solution(17954209683903541893)
XLA Ops:
  1.3 0.7 compare_and_fusion.1
  2.0 0.8 slice_bitcast_fusion.1
  2.7 0.7 compare_and_fusion
  3.5 0.7 and_select_fusion
  4.2 0.1 and.50
  4.4 0.8 pad_dynamic-slice_fusion
  5.2 0.1 reshape.182
  5.4 0.1 gt.15
  5.5 0.1 reshape.184
  5.6 0.7 broadcast_in_dim.41.pad_ref
  6.3 0.7 add_select_fusion.bias_ref
  7.0 0.1 broadcast_in_dim.40
  7.1 0.7 copy.21
  7.7 134.2 %shard_map.154 = (bf16[128,1536]{1,0:T(8,128)(2,1)}, bf16[128,1536]{1,0:T(8,128)(2,1)}, bf16[128,1536]{1,0:T(8,128)(2,1)}, bf16[128,1536]{1,0:T(8,128)(2,1)}, bf16[2,12,256,128]{3,2,1,0:T(8,128)(2,1)}) custom-call(bf16[128,1536]{1,0:T(8,128)(2,1)} %bitcast.30, bf16[128,1536]{1,0:T(8,128)(2,1)} %bitcast.31, bf16[128,1536]{1,0:T(8,128)(2,1)} %bitcast.32, ...), custom_call_target="tpu_custom_call" | custom-call | tf_op jit(solution)/shard_map/pallas_call | solution.py:463
  142.0 96.6 %shard_map.155 = (bf16[128,1536]{1,0:T(8,128)(2,1)}, bf16[128,1536]{1,0:T(8,128)(2,1)}, bf16[128,1536]{1,0:T(8,128)(2,1)}, bf16[128,1536]{1,0:T(8,128)(2,1)}, bf...) custom-call(bf16[128,1536]{1,0:T(8,128)(2,1)} %get-tuple-element.17.attn, bf16[128,1536]{1,0:T(8,128)(2,1)} %get-tuple-element.18.gq, ...), custom_call_target="tpu_custom_call" | custom-call | tf_op jit(solution)/shard_map/pallas_call | solution.py:503
  (8 shorter events, 0.1 us)

commit v2 on v1

v2 whole, which is shorter than its diff:
```python
import functools
import math

import jax
import jax.numpy as jnp
from jax import lax
from jax.experimental import pallas as pl
from jax.experimental.pallas import tpu as pltpu
from jax.sharding import PartitionSpec as P

HEADS = 12
HD = 128
TH = 8
TW = 8
TOK = 128
TEXT = 256
VID = 9 * TOK
KEYS = VID + TEXT
CH = HEADS * HD
GROUPS = 3
PER = HEADS // GROUPS
ROWS = TEXT // 8
SCALE = HD**-0.5
SCALE2 = SCALE * math.log2(math.e)
BIG = 1e30
MESH = pl.DeviceIdType.MESH
F32 = jnp.float32
BF16 = jnp.bfloat16
OFFSETS = tuple((dr, dc) for dr in (-1, 0, 1) for dc in (-1, 0, 1))


def dot_nt(a, b):
    return lax.dot_general(a, b, (((1,), (1,)), ((), ())), preferred_element_type=F32)


def dot_nn(a, b):
    return lax.dot_general(a, b, (((1,), (0,)), ((), ())), preferred_element_type=F32)


def dot_tn(a, b):
    return lax.dot_general(a, b, (((0,), (0,)), ((), ())), preferred_element_type=F32)


def cols(head):
    return pl.ds(pl.multiple_of(head * HD, HD), HD)


class Copy:
    def __init__(self, sems, number, src, dst, device, sends=None, receives=None):
        self.copy = pltpu.make_async_remote_copy(
            src_ref=src,
            dst_ref=dst,
            send_sem=sems[0].at[number],
            recv_sem=sems[1].at[number],
            device_id=device,
            device_id_type=MESH,
        )
        self.sends = sends
        self.receives = receives

    def start(self):
        if self.sends is None:
            self.copy.start()
        else:
            pl.when(self.sends)(self.copy.start)

    def wait_recv(self):
        if self.receives is None:
            self.copy.wait_recv()
        else:
            pl.when(self.receives)(self.copy.wait_recv)

    def wait_send(self):
        if self.sends is None:
            self.copy.wait_send()
        else:
            pl.when(self.sends)(self.copy.wait_send)


def regions(sizes):
    m_w, m_h = sizes
    c, b = HEADS - m_w, HEADS - m_h
    return (
        (range(0, c), (1, 4, 7)),
        (range(c, c + b), (3, 4, 5)),
        (range(c + b, HEADS), tuple(range(9))),
    )


def segments(sizes, step):
    runs = []
    for kind, (span, tiles) in enumerate(regions(sizes)):
        low = span.start
        while low < span.stop:
            high = min(span.stop, (low // step + 1) * step)
            runs.append((kind, low, high, tiles))
            low = high
    return runs


def main_kernel(
    sizes,
    kv_ref,
    qd_ref,
    text_in,
    bias_ref,
    qbias_ref,
    pad_ref,
    attn_ref,
    gq_ref,
    gk_ref,
    gv_ref,
    text_ref,
    kv_rw,
    kv_rh,
    kv_rc,
    qd_rw,
    qd_rh,
    qd_rc,
    left_ext,
    right_ext,
    stat_acc,
    stat_ext,
    own_part,
    pair_src,
    pair_dst,
    a_src,
    a_dst,
    z_acc,
    z_src,
    z_dst,
    b_all,
    send_sems,
    recv_sems,
):
    m_w, m_h = sizes
    n_c, n_b = HEADS - m_w, HEADS - m_h
    n_a = HEADS - n_c - n_b
    ha = lax.axis_index("ha")
    wa = lax.axis_index("wa")
    core = ha % 2
    x = (ha // 2) % 4
    y = (wa // 8) * 2 + ha // 8
    z = wa % 8

    def device(y_, x_, core_, z_):
        return ((y_ % 2) * 8 + x_ * 2 + core_, (y_ // 2) * 8 + z_)

    def a_partner(step):
        along = (core * x + (1 - core) * y + step) % 4
        return along, device(core * y + (1 - core) * along, core * along + (1 - core) * x, core, z)

    def b_partner(step):
        along = (core * y + (1 - core) * x + step) % 4
        return along, device(core * along + (1 - core) * y, core * x + (1 - core) * along, core, z)

    def z_partner(step):
        along = (z + step) % 8
        return along, device(y, x, core, along)

    a_me = core * x + (1 - core) * y
    b_me = core * y + (1 - core) * x
    pair = device(y, x, 1 - core, z)
    has = {-1: (ha > 0, wa > 0), 1: (ha < 15, wa < 15)}

    def exists(dr, dc):
        terms = [has[dr][0]] if dr else []
        terms += [has[dc][1]] if dc else []
        return functools.reduce(jnp.logical_and, terms)

    barrier = pltpu.get_barrier_semaphore()

    def greet(target):
        pl.semaphore_signal(barrier, inc=1, device_id=target, device_id_type=MESH)

    expected = jnp.int32(14)
    for dr, dc in OFFSETS:
        if dr or dc:
            there = exists(dr, dc)
            pl.when(there)(functools.partial(greet, (ha + dr, wa + dc)))
            expected = expected + there.astype(jnp.int32)
    for step in (1, 2, 3):
        greet(a_partner(step)[1])
        greet(b_partner(step)[1])
    for step in range(1, 8):
        greet(z_partner(step)[1])
    greet(pair)

    counter = [0]
    sems = (send_sems, recv_sems)

    def copy(src, dst, target, sends=None, receives=None):
        number = counter[0]
        counter[0] += 1
        return Copy(sems, number, src, dst, target, sends, receives)

    def blank(rw, rh, rc):
        for side, sign in ((0, -1), (1, 1)):

            @pl.when(jnp.logical_not(has[sign][1]))
            def _():
                rw[side] = jnp.zeros(rw.shape[1:], rw.dtype)

            @pl.when(jnp.logical_not(has[sign][0]))
            def _():
                rh[side] = jnp.zeros(rh.shape[1:], rh.dtype)
                rc[side] = jnp.zeros(rc.shape[1:], rc.dtype)

    def halo(own, rw, rh, rc):
        along_w, along_h, corner = [], [], []
        for side, sign in ((0, 1), (1, -1)):
            to, source = has[sign], has[-sign]
            along_w.append(
                copy(own.at[:, pl.ds(n_c, m_w)], rw.at[side], (ha, wa + sign), to[1], source[1])
            )
            for low, count, slot in ((0, n_c, 0), (n_c + n_b, n_a, n_c)):
                if count:
                    along_h.append(
                        copy(
                            own.at[:, pl.ds(low, count)],
                            rh.at[side, :, pl.ds(slot, count)],
                            (ha + sign, wa),
                            to[0],
                            source[0],
                        )
                    )
            corner.append(
                copy(rw.at[:, :, pl.ds(n_b, n_a)], rc.at[side], (ha + sign, wa), to[0], source[0])
            )
        return along_w, along_h, corner

    kv_w, kv_h, kv_c = halo(kv_ref, kv_rw, kv_rh, kv_rc)
    qd_w, qd_h, qd_c = halo(qd_ref, qd_rw, qd_rh, qd_rc)
    stat_copies = [
        copy(
            stat_ext.at[4],
            stat_ext.at[(1 - dr) * 3 + (1 - dc)],
            (ha + dr, wa + dc),
            exists(dr, dc),
            exists(-dr, -dc),
        )
        for dr, dc in OFFSETS
        if dr or dc
    ]

    pl.semaphore_wait(barrier, expected)
    for c in kv_h + kv_w:
        c.start()
    blank(kv_rw, kv_rh, kv_rc)
    blank(qd_rw, qd_rh, qd_rc)
    for dr, dc in OFFSETS:
        if dr or dc:

            @pl.when(jnp.logical_not(exists(dr, dc)))
            def _():
                stat_ext[(dr + 1) * 3 + dc + 1] = jnp.zeros((32, TOK), F32)

    def block(own_ref, index, rw, rh, rc, kind, position, tile):
        dr, dc = OFFSETS[tile]
        if dr == 0 and dc == 0:
            return own_ref[index, position]
        if dr == 0:
            return rw[(dc + 1) // 2, index, position - n_c]
        if dc == 0:
            return rh[(dr + 1) // 2, index, position if kind == 0 else position - n_b]
        return rc[(dr + 1) // 2, (dc + 1) // 2, index, position - n_c - n_b]

    def assemble(ext, first, own_ref, index, rw, rh, rc, kind, position, tiles):
        for i, tile in enumerate(tiles):
            ext[pl.ds(first + i * TOK, TOK), :] = block(
                own_ref, index, rw, rh, rc, kind, position, tile
            )

    lane = lax.broadcasted_iota(jnp.int32, (TOK, TOK), 1)

    def own_pass(kind, tiles, p):
        kv_halo = (kv_rw, kv_rh, kv_rc, kind, p, tiles)
        left_ext[pl.ds(0, TEXT), :] = text_in[0, p]
        right_ext[pl.ds(0, TEXT), :] = text_in[1, p]
        assemble(left_ext, TEXT, kv_ref, 0, *kv_halo)
        assemble(right_ext, TEXT, kv_ref, 1, *kv_halo)
        keys = left_ext[pl.ds(0, TEXT + len(tiles) * TOK), :]
        values = right_ext[pl.ds(0, TEXT + len(tiles) * TOK), :]
        query, grad = qd_ref[0, p], qd_ref[1, p]
        bias = jnp.concatenate([bias_ref[p, pl.ds(t, 1), :] for t in (9, 10) + tiles], axis=1)
        scores = dot_nt(query, keys) * SCALE2 + bias
        highest = jnp.max(scores, axis=1, keepdims=True)
        powers = jnp.exp2(scores - highest)
        total = jnp.sum(powers, axis=1, keepdims=True)
        probs = powers * (1.0 / total)
        probs_b = probs.astype(BF16)
        attn = dot_nn(probs_b, values).astype(BF16)
        attn_ref[p] = attn
        delta = jnp.sum(grad.astype(F32) * attn.astype(F32), axis=1, keepdims=True)
        slopes = (probs * (dot_nt(grad, values) - delta)).astype(BF16)
        gq_ref[p] = (SCALE * dot_nn(slopes, keys)).astype(BF16)
        log_total = highest + jnp.log(total) * math.log2(math.e)
        stat_acc[...] = jnp.where(
            lane == p, log_total, jnp.where(lane == p + 16, delta, stat_acc[...])
        )
        text_k = SCALE * dot_tn(slopes[:, :TEXT], query)
        text_v = dot_tn(probs_b[:, :TEXT], grad)
        own_part[p] = jnp.where(core == 0, text_k, text_v)
        pair_src[p] = jnp.where(core == 0, text_v, text_k).astype(BF16)

    def owner_pass(kind, tiles, p):
        qd_halo = (qd_rw, qd_rh, qd_rc, kind, p, tiles)
        assemble(left_ext, 0, qd_ref, 0, *qd_halo)
        assemble(right_ext, 0, qd_ref, 1, *qd_halo)
        log_total = jnp.concatenate(
            [stat_ext[t, pl.ds(p, 1), :] + qbias_ref[p, pl.ds(t, 1), :] for t in tiles], axis=1
        )
        delta = jnp.concatenate([stat_ext[t, pl.ds(p + 16, 1), :] for t in tiles], axis=1)
        queries = left_ext[pl.ds(0, len(tiles) * TOK), :]
        grads = right_ext[pl.ds(0, len(tiles) * TOK), :]
        probs = jnp.exp2(dot_nt(kv_ref[0, p], queries) * SCALE2 - log_total)
        slopes = (probs * (dot_nt(kv_ref[1, p], grads) - delta)).astype(BF16)
        real = pad_ref[...] > 0
        gk_ref[p] = jnp.where(real, SCALE * dot_nn(slopes, queries), 0.0).astype(BF16)
        gv_ref[p] = jnp.where(real, dot_nn(probs.astype(BF16), grads), 0.0).astype(BF16)

    started = []

    def stage_pair(g):
        span = pl.ds(g * PER, PER)
        made = [copy(pair_src.at[span], pair_dst.at[span], pair)]
        return made, None

    def prepare_a(g):
        for i in range(PER):
            own_part[g * PER + i] = own_part[g * PER + i] + pair_dst[g * PER + i].astype(F32)

        made = []
        for step in (1, 2, 3):
            along, target = a_partner(step)
            a_src[g, step - 1] = own_part[g * PER + along].astype(BF16)
            made.append(copy(a_src.at[g, step - 1], a_dst.at[g, step - 1], target))
        return made

    def prepare_z(g):
        z_acc[g] = (
            own_part[g * PER + a_me]
            + a_dst[g, 0].astype(F32)
            + a_dst[g, 1].astype(F32)
            + a_dst[g, 2].astype(F32)
        )
        z_src[g] = z_acc[g].astype(BF16)
        made = []
        for step in range(1, 8):
            along, target = z_partner(step)
            rows = pl.ds(pl.multiple_of(along * ROWS, ROWS), ROWS)
            made.append(copy(z_src.at[g, rows], z_dst.at[g, step - 1], target))
        return made

    def prepare_b(g):
        total = z_acc[g, pl.ds(pl.multiple_of(z * ROWS, ROWS), ROWS), :]
        for step in range(7):
            total = total + z_dst[g, step].astype(F32)
        b_all[g, b_me] = total.astype(BF16)
        return [
            copy(b_all.at[g, b_me], b_all.at[g, b_me], b_partner(step)[1]) for step in (1, 2, 3)
        ]

    def prepare_z_back(g):
        total = b_all[g, 0].astype(F32)
        for i in (1, 2, 3):
            total = total + b_all[g, i].astype(F32)
        rows = pl.ds(pl.multiple_of(z * ROWS, ROWS), ROWS)
        piece = text_ref.at[core, g * PER + a_me, rows]
        text_ref[core, g * PER + a_me, rows, :] = total.astype(BF16)
        return [copy(piece, piece, z_partner(step)[1]) for step in range(1, 8)]

    def prepare_a_back(g):
        piece = text_ref.at[core, g * PER + a_me]
        return [copy(piece, piece, a_partner(step)[1]) for step in (1, 2, 3)]

    def prepare_pair_back(g):
        piece = text_ref.at[core, pl.ds(g * PER, PER)]
        return [copy(piece, piece, pair)]

    stages = (
        lambda g: stage_pair(g)[0],
        prepare_a,
        prepare_z,
        prepare_b,
        prepare_z_back,
        prepare_a_back,
        prepare_pair_back,
        lambda g: [],
    )
    flying = [[] for _ in range(GROUPS)]
    level = [0] * GROUPS

    def advance(g):
        if level[g] >= len(stages):
            return
        for c in flying[g]:
            c.wait_recv()
        flying[g] = stages[level[g]](g)
        level[g] += 1
        for c in flying[g]:
            c.start()
        started.extend(flying[g])

    stat_acc[...] = jnp.zeros((TOK, TOK), F32)
    for c in kv_h:
        c.wait_recv()
    for c in qd_h:
        c.start()

    done = set()

    def once(name, action):
        if name not in done:
            done.add(name)
            action()

    def take_kv_w():
        for c in kv_w:
            c.wait_recv()
        for c in kv_c + qd_w:
            c.start()

    def take_kv_c():
        for c in kv_c:
            c.wait_recv()

    for kind, low, high, tiles in segments(sizes, PER):
        if kind >= 1:
            once("kv_w", take_kv_w)
        if kind == 2:
            once("kv_c", take_kv_c)

        @pl.loop(low, high)
        def _(p):
            own_pass(kind, tiles, p)

        if high % PER == 0:
            if high == HEADS:
                stat_ext[4] = jnp.transpose(stat_acc[...])[:32]
                for c in stat_copies:
                    c.start()
            for earlier in range(high // PER):
                advance(earlier)

    for c in qd_w:
        c.wait_recv()
    for c in qd_c:
        c.start()
    for c in qd_h + stat_copies:
        c.wait_recv()
    for kind, low, high, tiles in segments(sizes, 2):
        if kind == 2:
            once("qd_c", lambda: [c.wait_recv() for c in qd_c])
        for g in range(GROUPS):
            advance(g)

        @pl.loop(low, high)
        def _(p):
            owner_pass(kind, tiles, p)

    for _ in stages:
        for g in range(GROUPS):
            advance(g)
    for c in kv_w + kv_h + kv_c + qd_w + qd_h + qd_c + stat_copies + started:
        c.wait_send()
    assert counter[0] <= N_COPIES


N_COPIES = 24 + GROUPS * 25


def finish_kernel(place, attn, gq, gk, gv, text, o_attn, o_gq, o_gk, o_gv, o_tk, o_tv):
    for h in range(HEADS):
        p = place[h]
        for source, out in ((attn, o_attn), (gq, o_gq), (gk, o_gk), (gv, o_gv)):
            out[:, h * HD : (h + 1) * HD] = source[p]
        for side, out in ((0, o_tk), (1, o_tv)):
            out[:, h * HD : (h + 1) * HD] = text[side, p]


VMEM = pl.BlockSpec(memory_space=pltpu.VMEM)
SMEM = pl.BlockSpec(memory_space=pltpu.SMEM)


def fused(number, sizes, operands):
    m_w, m_h = sizes
    n_a = m_w + m_h - HEADS
    halo = [
        pltpu.VMEM((2, 2, m_w, TOK, HD), BF16),
        pltpu.VMEM((2, 2, m_h, TOK, HD), BF16),
        pltpu.VMEM((2, 2, 2, n_a, TOK, HD), BF16),
    ]
    token = jax.ShapeDtypeStruct((HEADS, TOK, HD), BF16)
    return pl.pallas_call(
        functools.partial(main_kernel, sizes),
        out_shape=(token,) * 4 + (jax.ShapeDtypeStruct((2, HEADS, TEXT, HD), BF16),),
        in_specs=[VMEM] * 6,
        out_specs=(VMEM,) * 5,
        scratch_shapes=halo
        + halo
        + [
            pltpu.VMEM((KEYS, HD), BF16),
            pltpu.VMEM((KEYS, HD), BF16),
            pltpu.VMEM((TOK, TOK), F32),
            pltpu.VMEM((9, 32, TOK), F32),
            pltpu.VMEM((HEADS, TEXT, HD), F32),
            pltpu.VMEM((HEADS, TEXT, HD), BF16),
            pltpu.VMEM((HEADS, TEXT, HD), BF16),
            pltpu.VMEM((GROUPS, 3, TEXT, HD), BF16),
            pltpu.VMEM((GROUPS, 3, TEXT, HD), BF16),
            pltpu.VMEM((GROUPS, TEXT, HD), F32),
            pltpu.VMEM((GROUPS, TEXT, HD), BF16),
            pltpu.VMEM((GROUPS, 7, ROWS, HD), BF16),
            pltpu.VMEM((GROUPS, 4, ROWS, HD), BF16),
            pltpu.SemaphoreType.DMA((N_COPIES,)),
            pltpu.SemaphoreType.DMA((N_COPIES,)),
        ],
        compiler_params=pltpu.CompilerParams(
            collective_id=number, has_side_effects=True, vmem_limit_bytes=56 * 1024 * 1024
        ),
    )(*operands)


def finish(place, results):
    token = jax.ShapeDtypeStruct((TOK, CH), BF16)
    rows = jax.ShapeDtypeStruct((TEXT, CH), BF16)
    return pl.pallas_call(
        finish_kernel,
        out_shape=(token, token, token, token, rows, rows),
        in_specs=[SMEM] + [VMEM] * 5,
        out_specs=(VMEM,) * 6,
        compiler_params=pltpu.CompilerParams(vmem_limit_bytes=16 * 1024 * 1024),
    )(place, *results)


def count_of(flags):
    return functools.reduce(jnp.add, flags)


def ready_kernel(
    reach, live, q, k, v, d, tk, tv, mask, kv, qd, text, bias, qbias, pad, place, choice
):
    ha = lax.axis_index("ha")
    wa = lax.axis_index("wa")
    high = [reach[h, 0] for h in range(HEADS)]
    wide = [reach[h, 1] for h in range(HEADS)]
    both = [high[h] * wide[h] for h in range(HEADS)]
    only_h = [high[h] - both[h] for h in range(HEADS)]
    only_w = [wide[h] - both[h] for h in range(HEADS)]
    n_both, n_h, n_w = count_of(both), count_of(only_h), count_of(only_w)

    m_w, m_h, number = jnp.int32(HEADS), jnp.int32(HEADS), jnp.int32(len(VARIANTS) - 1)
    for i in reversed(range(len(VARIANTS) - 1)):
        w, h = VARIANTS[i]
        need = n_both + jnp.maximum(n_w - (HEADS - h), 0) + jnp.maximum(n_h - (HEADS - w), 0)
        fits = need <= w + h - HEADS
        m_w = jnp.where(fits, w, m_w)
        m_h = jnp.where(fits, h, m_h)
        number = jnp.where(fits, i, number)
    choice[0] = number
    room_h, room_w = HEADS - m_w, HEADS - m_h
    in_h, in_w = jnp.minimum(n_h, room_h), jnp.minimum(n_w, room_w)
    first_both = room_h + room_w
    spill_w = first_both + n_both
    spill_h = spill_w + n_w - in_w
    rest = spill_h + n_h - in_h

    seen_both = seen_h = seen_w = seen_none = jnp.int32(0)
    for h in range(HEADS):
        at_h = jnp.where(seen_h < room_h, seen_h, spill_h + seen_h - room_h)
        at_w = jnp.where(seen_w < room_w, room_h + seen_w, spill_w + seen_w - room_w)
        left_h, left_w = room_h - in_h, room_w - in_w
        at_none = jnp.where(
            seen_none < left_h,
            in_h + seen_none,
            jnp.where(
                seen_none < left_h + left_w,
                room_h + in_w + seen_none - left_h,
                rest + seen_none - left_h - left_w,
            ),
        )
        at = jnp.where(
            both[h] == 1,
            first_both + seen_both,
            jnp.where(only_h[h] == 1, at_h, jnp.where(only_w[h] == 1, at_w, at_none)),
        )
        place[h] = at
        seen_both = seen_both + both[h]
        seen_h = seen_h + only_h[h]
        seen_w = seen_w + only_w[h]
        seen_none = seen_none + 1 - both[h] - only_h[h] - only_w[h]

    line = lax.broadcasted_iota(jnp.int32, (TOK, TOK), 0)
    lane = lax.broadcasted_iota(jnp.int32, (TOK, TOK), 1)
    slabs = []
    for dr in (-1, 0, 1):
        row = jnp.clip(ha + dr, 0, 15)
        there = (ha + dr >= 0) & (ha + dr < 16)
        for f in range(2):
            slab = mask[f, pl.ds(pl.multiple_of(row * TH, TH), TH), :]
            slabs.append(jnp.where(there, slab, 0))
    slabs = jnp.concatenate(slabs, axis=0).astype(F32)
    pick = (lax.broadcasted_iota(jnp.int32, (TH, TOK), 1) // TW) % TH
    pick = pick == lax.broadcasted_iota(jnp.int32, (TH, TOK), 0)
    frame = lax.broadcasted_iota(jnp.int32, (1, TOK), 1) // (TH * TW)
    rows = [[None] * 3 for _ in range(3)]
    for j, dc in enumerate((-1, 0, 1)):
        chosen = (line == (wa + dc) * TW + lane % TW).astype(F32)
        spread = jnp.dot(slabs, chosen, preferred_element_type=F32)
        for i in range(3):
            parts = [
                jnp.sum(
                    jnp.where(pick, spread[(i * 2 + f) * TH : (i * 2 + f + 1) * TH], 0.0),
                    axis=0,
                    keepdims=True,
                )
                for f in range(2)
            ]
            rows[i][j] = jnp.where(frame == 0, parts[0], parts[1])
    nine = [rows[i][j] for i in range(3) for j in range(3)]
    column = lax.broadcasted_iota(jnp.int32, (1, TOK), 1)
    words = [(column + i * TOK < live[0]).astype(F32) for i in range(2)]
    table = jnp.concatenate(nine + words + [jnp.zeros((5, TOK), F32)], axis=0)
    pad[...] = jnp.transpose(jnp.broadcast_to(nine[4], (TOK, TOK)))

    tile = lax.broadcasted_iota(jnp.int32, (16, TOK), 0)
    dr, dc = tile // 3 - 1, tile % 3 - 1
    there = (ha + dr >= 0) & (ha + dr < 16) & (wa + dc >= 0) & (wa + dc < 16)
    for h in range(HEADS):
        p = place[h]
        inside = (jnp.abs(dr) <= high[h]) & (jnp.abs(dc) <= wide[h])
        bias[p] = jnp.where((table > 0.5) & (inside | (tile >= 9)), 0.0, -BIG)
        qbias[p] = jnp.where(inside & there, 0.0, BIG)
        for source, out, index in ((k, kv, 0), (v, kv, 1), (q, qd, 0), (d, qd, 1)):
            out[index, p] = source[:, h * HD : (h + 1) * HD]
        for source, index in ((tk, 0), (tv, 1)):
            text[index, p] = source[:, h * HD : (h + 1) * HD]


def ready(reach, live, q, k, v, d, tk, tv, mask):
    tokens = jax.ShapeDtypeStruct((2, HEADS, TOK, HD), BF16)
    rows = jax.ShapeDtypeStruct((HEADS, 16, TOK), F32)
    return pl.pallas_call(
        ready_kernel,
        out_shape=(
            tokens,
            tokens,
            jax.ShapeDtypeStruct((2, HEADS, TEXT, HD), BF16),
            rows,
            rows,
            jax.ShapeDtypeStruct((TOK, TOK), F32),
            jax.ShapeDtypeStruct((HEADS,), jnp.int32),
            jax.ShapeDtypeStruct((1,), jnp.int32),
        ),
        in_specs=[SMEM, SMEM] + [VMEM] * 7,
        out_specs=(VMEM,) * 6 + (SMEM, SMEM),
        compiler_params=pltpu.CompilerParams(vmem_limit_bytes=24 * 1024 * 1024),
    )(reach, live, q, k, v, d, tk, tv, mask)


VARIANTS = ((7, 8), (9, 9), (HEADS, HEADS))


def body(
    query_tokens,
    key_tokens,
    value_tokens,
    grad_output,
    text_keys,
    text_values,
    reach_tiles,
    text_count,
    pad_mask,
):
    shape = query_tokens.shape
    tokens = [t.reshape(TOK, CH) for t in (query_tokens, key_tokens, value_tokens, grad_output)]
    *operands, place, choice = ready(
        reach_tiles, text_count, *tokens, text_keys, text_values, pad_mask
    )

    def variant(number, sizes):
        return lambda place, *operands: finish(place, fused(number, sizes, operands))

    attn, gq, gk, gv, tk, tv = lax.switch(
        choice[0],
        [variant(number, sizes) for number, sizes in enumerate(VARIANTS)],
        place,
        *operands,
    )
    return (
        attn.reshape(shape),
        gq.reshape(shape),
        gk.reshape(shape),
        gv.reshape(shape),
        tk,
        tv,
    )


def solution(mesh):
    tokens = P(None, "ha", "wa", None)
    return jax.shard_map(
        body,
        mesh=mesh,
        in_specs=(tokens,) * 4 + (P(),) * 5,
        out_specs=(tokens,) * 4 + (P(), P()),
        check_vma=False,
    )
```

time: 239 us -> 106 us (0.44)
  Pallas kernels: 231 us -> 90.6 us
  local copies, waits for them, and re-layouts: 3.49 us -> 13.3 us
  other arithmetic: 2.88 us -> 0 us
    pallas_call x1, Pallas kernels: 96.6 us -> 2.75 us  [finish(): pl.pallas_call(finish_kernel, out_shape=(token, token, token, token, rows...]
    pallas_call x1 -> x2, Pallas kernels: 134 us -> 87.8 us  [the longest x1 85.8 us: fused(): pl.pallas_call(functools.partial(main_kernel, sizes), out_shape=(token,)...]
    unnamed x4 -> x15, local copies, waits for them, and re-layouts: 0.7 us -> 7.92 us
    cond x0 -> x10, local copies, waits for them, and re-layouts: none -> 5.38 us
where the time goes in v2:
time: 106 us
  Pallas kernels  90.6 us (85%)
  local copies, waits for them, and re-layouts  13.3 us (13%)
  between operations  1.94 us (2%)
    pallas_call x1, Pallas kernels, fused(): pl.pallas_call(functools.partial(main_kernel, sizes), out_shape=(token,)...  85.8 us
    unnamed x15, local copies, waits for them, and re-layouts  7.92 us
    cond x10, local copies, waits for them, and re-layouts  5.38 us
    pallas_call x1, Pallas kernels, finish(): pl.pallas_call(finish_kernel, out_shape=(token, token, token, token, rows...  2.75 us

profile of v2, /device:TPU:1, one launch (start us, length us, event | category | flops | bytes accessed | tf_op | source)
XLA Modules:
  0.0 105.8 jit_solution(2322446739688014623)
XLA Ops:
  1.3 0.8 copy.15.reach
  2.0 0.0 copy-start.3
  2.0 1.1 %copy-done.3 = bf16[256,1536]{1,0:T(8,128)(2,1)S(1)} copy-done((bf16[256,1536]{1,0:T(8,128)(2,1)S(1)}, bf16[256,1536]{1,0:T(8,128)(2,1)}, u32[]{:S(2)}) %copy-start.3) | copy-done | bytes 786456
  3.2 0.0 copy-start.4
  3.2 1.1 %copy-done.4 = bf16[256,1536]{1,0:T(8,128)(2,1)S(1)} copy-done((bf16[256,1536]{1,0:T(8,128)(2,1)S(1)}, bf16[256,1536]{1,0:T(8,128)(2,1)}, u32[]{:S(2)}) %copy-start.4) | copy-done | bytes 786456
  4.3 0.0 copy-start.5
  4.3 1.0 copy-done.5
  5.3 0.0 copy-start.6
  5.3 1.0 copy-done.6
  6.3 0.0 copy-start.7
  6.3 1.0 copy-done.7
  7.3 0.0 copy-start.8
  7.3 1.0 copy-done.8
  8.3 0.0 copy-start.21
  8.3 0.9 copy-done.21
  9.2 2.0 %shard_map.136 = (bf16[2,12,128,128]{3,2,1,0:T(8,128)(2,1)S(1)}, bf16[2,12,128,128]{3,2,1,0:T(8,128)(2,1)S(1)}, bf16[2,12,256,128]{3,2,1,0:T(8,128)(2,1)S(1)}, f...) custom-call(s32[12,2]{1,0:T(8,128)S(1)} %copy.15.reach, ...), custom_call_target="tpu_custom_call" | custom-call | tf_op jit(solution)/shard_map/pallas_call | solution.py:644
  11.9 93.9 %conditional.1 = ((bf16[128,1536]{1,0:T(8,128)(2,1)}, bf16[128,1536]{1,0:T(8,128)(2,1)}, bf16[128,1536]{1,0:T(8,128)(2,1)}, bf16[128,1536]{1,0:T(8,128)(2,1)}, b...) conditional(s32[]{:T(128)} %bitcast.4, ...), branch_computations={%region_0.0_spmd.clone, %region_1.0_spmd.clone, %region_2.0_spmd.c... | conditional | bytes 12583060 | solution.py:685
  11.9 85.8 %branch_0_fun.4 = (bf16[12,128,128]{2,1,0:T(8,128)(2,1)}, bf16[12,128,128]{2,1,0:T(8,128)(2,1)}, bf16[12,128,128]{2,1,0:T(8,128)(2,1)}, bf16[12,128,128]{2,1,0:T(8,128)(2,1)}, bf16[2,12,256,128]{3,2,1,0:T(8,128)(2,1)}) custom-call(bf16[2,12,128,128]{3,2,1,0:T(8,128)(2,1)S(1)} %get-tuple-element.176.kv_ref, ...), custom_call_target="tpu_custom_call" | custom-call | tf_op jit(solution)/shard_map/cond/branch_0_fun/pallas_call | solution.py:495
  97.7 0.0 copy-start
  97.7 1.4 %copy-done = bf16[2,12,256,128]{3,2,1,0:T(8,128)(2,1)S(1)} copy-done((bf16[2,12,256,128]{3,2,1,0:T(8,128)(2,1)S(1)}, bf16[2,12,256,128]{3,2,1,0:T(8,128)(2,1)}, u32[]{:S(2)}) %copy-start) | copy-done | bytes 1572888 | tf_op jit(solution)/shard_map/cond
  99.1 0.0 copy-start.9
  99.1 1.0 copy-done.9
  100.1 0.0 copy-start.10
  100.1 1.0 copy-done.10
  101.1 0.0 copy-start.11
  101.1 1.0 copy-done.11
  102.1 0.0 copy-start.12
  102.1 1.0 copy-done.12
  103.1 2.7 %branch_0_fun.5 = (bf16[128,1536]{1,0:T(8,128)(2,1)}, bf16[128,1536]{1,0:T(8,128)(2,1)}, bf16[128,1536]{1,0:T(8,128)(2,1)}, bf16[128,1536]{1,0:T(8,128)(2,1)}, b...) custom-call(s32[12]{0:T(128)S(1)} %get-tuple-element.175.place, bf16[12,128,128]{2,1,0:T(8,128)(2,1)S(1)} %copy-done.9, ...), custom_call_target="tpu_custom_call" | custom-call | tf_op jit(solution)/shard_map/cond/branch_0_fun/pallas_call | solution.py:528
Async XLA Ops:
  2.0 1.1 %copy-start.3 = (bf16[256,1536]{1,0:T(8,128)(2,1)S(1)}, bf16[256,1536]{1,0:T(8,128)(2,1)}, u32[]{:S(2)}) copy-start(bf16[256,1536]{1,0:T(8,128)(2,1)} %tk.1) | copy-start | bytes 2359300
  3.2 1.1 %copy-start.4 = (bf16[256,1536]{1,0:T(8,128)(2,1)S(1)}, bf16[256,1536]{1,0:T(8,128)(2,1)}, u32[]{:S(2)}) copy-start(bf16[256,1536]{1,0:T(8,128)(2,1)} %tv.1) | copy-start | bytes 2359300
  4.3 1.0 copy-start.5
  5.3 1.0 copy-start.6
  6.3 1.0 copy-start.7
  7.3 1.0 copy-start.8
  8.3 0.9 copy-start.21
  97.7 1.4 %copy-start = (bf16[2,12,256,128]{3,2,1,0:T(8,128)(2,1)S(1)}, bf16[2,12,256,128]{3,2,1,0:T(8,128)(2,1)}, u32[]{:S(2)}) copy-start(bf16[2,12,256,128]{3,2,1,0:T(8,128)(2,1)} %get-tuple-element.186.text) | copy-start | bytes 4718596 | tf_op jit(solution)/shard_map/cond
  99.1 1.0 copy-start.9
  100.1 1.0 copy-start.10
  101.1 1.0 copy-start.11
  102.1 1.0 copy-start.12

commit v3 on v2

--- a/solution.py
+++ b/solution.py
@@ -20,6 +20,7 @@
 GROUPS = 3
 PER = HEADS // GROUPS
 ROWS = TEXT // 8
+IDLE_ROUNDS = 0
 SCALE = HD**-0.5
 SCALE2 = SCALE * math.log2(math.e)
 BIG = 1e30
@@ -405,8 +406,6 @@
     stat_acc[...] = jnp.zeros((TOK, TOK), F32)
     for c in kv_h:
         c.wait_recv()
-    for c in qd_h:
-        c.start()
 
     done = set()
 
@@ -418,10 +417,13 @@
     def take_kv_w():
         for c in kv_w:
             c.wait_recv()
-        for c in kv_c + qd_w:
+        for c in kv_c + qd_w + qd_h:
             c.start()
 
     def take_kv_c():
+        for _ in range(IDLE_ROUNDS):
+            for g in range((n_c + n_b) // PER):
+                advance(g)
         for c in kv_c:
             c.wait_recv()
 
@@ -440,19 +442,23 @@
                 stat_ext[4] = jnp.transpose(stat_acc[...])[:32]
                 for c in stat_copies:
                     c.start()
-            for earlier in range(high // PER):
+            for earlier in reversed(range(high // PER)):
                 advance(earlier)
 
+    for g in reversed(range(GROUPS)):
+        advance(g)
     for c in qd_w:
         c.wait_recv()
     for c in qd_c:
         c.start()
+    for g in reversed(range(GROUPS)):
+        advance(g)
     for c in qd_h + stat_copies:
         c.wait_recv()
     for kind, low, high, tiles in segments(sizes, 2):
         if kind == 2:
             once("qd_c", lambda: [c.wait_recv() for c in qd_c])
-        for g in range(GROUPS):
+        for g in reversed(range(GROUPS)):
             advance(g)
 
         @pl.loop(low, high)
@@ -470,17 +476,27 @@
 N_COPIES = 24 + GROUPS * 25
 
 
-def finish_kernel(place, attn, gq, gk, gv, text, o_attn, o_gq, o_gk, o_gv, o_tk, o_tv):
-    for h in range(HEADS):
-        p = place[h]
-        for source, out in ((attn, o_attn), (gq, o_gq), (gk, o_gk), (gv, o_gv)):
-            out[:, h * HD : (h + 1) * HD] = source[p]
-        for side, out in ((0, o_tk), (1, o_tv)):
-            out[:, h * HD : (h + 1) * HD] = text[side, p]
+def finish_kernel(
+    place, attn, gq, gk, gv, text, o_attn, o_gq, o_gk, o_gv, o_tk, o_tv, tokens, words, sems
+):
+    moves = []
+    for i, (source, out) in enumerate(((attn, o_attn), (gq, o_gq), (gk, o_gk), (gv, o_gv))):
+        for h in range(HEADS):
+            tokens[i, :, h * HD : (h + 1) * HD] = source[place[h]]
+        moves.append(pltpu.make_async_copy(tokens.at[i], out, sems.at[i]))
+        moves[-1].start()
+    for i, out in enumerate((o_tk, o_tv)):
+        for h in range(HEADS):
+            words[i, :, h * HD : (h + 1) * HD] = text[i, place[h]]
+        moves.append(pltpu.make_async_copy(words.at[i], out, sems.at[4 + i]))
+        moves[-1].start()
+    for move in moves:
+        move.wait()
 
 
 VMEM = pl.BlockSpec(memory_space=pltpu.VMEM)
 SMEM = pl.BlockSpec(memory_space=pltpu.SMEM)
+HBM = pl.BlockSpec(memory_space=pltpu.HBM)
 
 
 def fused(number, sizes, operands):
@@ -517,7 +533,7 @@
             pltpu.SemaphoreType.DMA((N_COPIES,)),
         ],
         compiler_params=pltpu.CompilerParams(
-            collective_id=number, has_side_effects=True, vmem_limit_bytes=56 * 1024 * 1024
+            collective_id=number, has_side_effects=True, vmem_limit_bytes=40 * 1024 * 1024
         ),
     )(*operands)
 
@@ -529,7 +545,12 @@
         finish_kernel,
         out_shape=(token, token, token, token, rows, rows),
         in_specs=[SMEM] + [VMEM] * 5,
-        out_specs=(VMEM,) * 6,
+        out_specs=(HBM,) * 6,
+        scratch_shapes=[
+            pltpu.VMEM((4, TOK, CH), BF16),
+            pltpu.VMEM((2, TEXT, CH), BF16),
+            pltpu.SemaphoreType.DMA((6,)),
+        ],
         compiler_params=pltpu.CompilerParams(vmem_limit_bytes=16 * 1024 * 1024),
     )(place, *results)
 
@@ -539,8 +560,46 @@
 
 
 def ready_kernel(
-    reach, live, q, k, v, d, tk, tv, mask, kv, qd, text, bias, qbias, pad, place, choice
+    reach,
+    live,
+    q_hbm,
+    k_hbm,
+    v_hbm,
+    d_hbm,
+    tk_hbm,
+    tv_hbm,
+    mask_hbm,
+    kv,
+    qd,
+    text,
+    bias,
+    qbias,
+    pad,
+    place,
+    choice,
+    mask,
+    tokens,
+    words,
+    sems,
 ):
+    k, v, q, d = (tokens.at[i] for i in range(4))
+    tk, tv = (words.at[i] for i in range(2))
+    moves = [
+        pltpu.make_async_copy(source, target, sems.at[i])
+        for i, (source, target) in enumerate(
+            (
+                (mask_hbm, mask),
+                (k_hbm, k),
+                (v_hbm, v),
+                (q_hbm, q),
+                (d_hbm, d),
+                (tk_hbm, tk),
+                (tv_hbm, tv),
+            )
+        )
+    ]
+    for move in moves:
+        move.start()
     ha = lax.axis_index("ha")
     wa = lax.axis_index("wa")
     high = [reach[h, 0] for h in range(HEADS)]
@@ -591,6 +650,7 @@
         seen_w = seen_w + only_w[h]
         seen_none = seen_none + 1 - both[h] - only_h[h] - only_w[h]
 
+    moves[0].wait()
     line = lax.broadcasted_iota(jnp.int32, (TOK, TOK), 0)
     lane = lax.broadcasted_iota(jnp.int32, (TOK, TOK), 1)
     slabs = []
@@ -632,10 +692,12 @@
         inside = (jnp.abs(dr) <= high[h]) & (jnp.abs(dc) <= wide[h])
         bias[p] = jnp.where((table > 0.5) & (inside | (tile >= 9)), 0.0, -BIG)
         qbias[p] = jnp.where(inside & there, 0.0, BIG)
-        for source, out, index in ((k, kv, 0), (v, kv, 1), (q, qd, 0), (d, qd, 1)):
-            out[index, p] = source[:, h * HD : (h + 1) * HD]
-        for source, index in ((tk, 0), (tv, 1)):
-            text[index, p] = source[:, h * HD : (h + 1) * HD]
+    for i, (source, out, index) in enumerate(
+        ((k, kv, 0), (v, kv, 1), (q, qd, 0), (d, qd, 1), (tk, text, 0), (tv, text, 1))
+    ):
+        moves[i + 1].wait()
+        for h in range(HEADS):
+            out[index, place[h]] = source[:, h * HD : (h + 1) * HD]
 
 
 def ready(reach, live, q, k, v, d, tk, tv, mask):
@@ -653,10 +715,16 @@
             jax.ShapeDtypeStruct((HEADS,), jnp.int32),
             jax.ShapeDtypeStruct((1,), jnp.int32),
         ),
-        in_specs=[SMEM, SMEM] + [VMEM] * 7,
+        in_specs=[SMEM, SMEM] + [HBM] * 7,
         out_specs=(VMEM,) * 6 + (SMEM, SMEM),
+        scratch_shapes=[
+            pltpu.VMEM((2, 128, 128), jnp.int32),
+            pltpu.VMEM((4, TOK, CH), BF16),
+            pltpu.VMEM((2, TEXT, CH), BF16),
+            pltpu.SemaphoreType.DMA((7,)),
+        ],
         compiler_params=pltpu.CompilerParams(vmem_limit_bytes=24 * 1024 * 1024),
-    )(reach, live, q, k, v, d, tk, tv, mask)
+    )(reach, live, *(pltpu.with_memory_space_constraint(x, pltpu.HBM) for x in (q, k, v, d, tk, tv, mask)))
 
 
 VARIANTS = ((7, 8), (9, 9), (HEADS, HEADS))

time: 106 us -> 108 us (1.019)
  Pallas kernels: 90.6 us -> 104 us
  local copies, waits for them, and re-layouts: 13.3 us -> 0.77 us
    pallas_call x1, Pallas kernels: 85.8 us -> 98.5 us  [fused(): pl.pallas_call(functools.partial(main_kernel, sizes), out_shape=(token,)...]
    unnamed x15 -> x1, local copies, waits for them, and re-layouts: 7.92 us -> 0.77 us
    cond x10 -> x0, local copies, waits for them, and re-layouts: 5.38 us -> none
    pallas_call x1, Pallas kernels: 2.05 us -> 3.38 us  [ready(): pl.pallas_call(ready_kernel, out_shape=(tokens, tokens, jax.ShapeDtypeStr...]
where the time goes in v3:
time: 108 us
  Pallas kernels  104 us (96%)
  between operations  2.12 us (2%)
    pallas_call x1, Pallas kernels, fused(): pl.pallas_call(functools.partial(main_kernel, sizes), out_shape=(token,)...  98.5 us
    pallas_call x1, Pallas kernels, ready(): pl.pallas_call(ready_kernel, out_shape=(tokens, tokens, jax.ShapeDtypeStr...  3.38 us
    pallas_call x1, Pallas kernels, finish(): pl.pallas_call(finish_kernel, out_shape=(token, token, token, token, rows...  2.33 us

profile of v3, /device:TPU:1, one launch (start us, length us, event | category | flops | bytes accessed | tf_op | source)
XLA Modules:
  0.0 107.6 jit_solution(3593049118534273841)
XLA Ops:
  1.3 0.8 copy.15.reach
  2.0 3.4 %shard_map.136 = (bf16[2,12,128,128]{3,2,1,0:T(8,128)(2,1)S(1)}, bf16[2,12,128,128]{3,2,1,0:T(8,128)(2,1)S(1)}, bf16[2,12,256,128]{3,2,1,0:T(8,128)(2,1)S(1)}, f...) custom-call(s32[12,2]{1,0:T(8,128)S(1)} %copy.15.reach, ...), custom_call_target="tpu_custom_call" | custom-call | tf_op jit(solution)/shard_map/pallas_call | solution.py:706
  6.1 101.4 %conditional.1 = ((bf16[128,1536]{1,0:T(8,128)(2,1)}, bf16[128,1536]{1,0:T(8,128)(2,1)}, bf16[128,1536]{1,0:T(8,128)(2,1)}, bf16[128,1536]{1,0:T(8,128)(2,1)}, b...) conditional(s32[]{:T(128)} %bitcast.4, ...), branch_computations={%region_0.0_spmd.clone, %region_1.0_spmd.clone, %region_2.0_spmd.c... | conditional | bytes 8 | solution.py:753
  6.1 98.5 %branch_1_fun.4 = (bf16[12,128,128]{2,1,0:T(8,128)(2,1)S(1)}, bf16[12,128,128]{2,1,0:T(8,128)(2,1)S(1)}, bf16[12,128,128]{2,1,0:T(8,128)(2,1)S(1)}, bf16[12,128,...) custom-call(bf16[2,12,128,128]{3,2,1,0:T(8,128)(2,1)S(1)} %get-tuple-element.189.kv_ref, ...), custom_call_target="tpu_custom_call" | custom-call | tf_op jit(solution)/shard_map/cond/branch_1_fun/pallas_call | solution.py:511
  104.6 2.3 %branch_1_fun.5 = (bf16[128,1536]{1,0:T(8,128)(2,1)}, bf16[128,1536]{1,0:T(8,128)(2,1)}, bf16[128,1536]{1,0:T(8,128)(2,1)}, bf16[128,1536]{1,0:T(8,128)(2,1)}, b...) custom-call(s32[12]{0:T(128)S(1)} %get-tuple-element.188.place, bf16[12,128,128]{2,1,0:T(8,128)(2,1)S(1)} %get-tuple-element.195.attn, ...), custom_call_target="tpu_custom_call" | custom-call | tf_op jit(solution)/shard_map/cond/branch_1_fun/pallas_call | solution.py:544
